TPU v7x, 256 devices: a whole 4x4x8 slice. The times are simulated.
256 devices in a mesh: gz: 8 (over y, x_hi), gy: 8 (over z), gx: 4 (over x_lo, core).
Axes of the slice: x: 4 (x_hi: 2, x_lo: 2; x = x_hi * 2 + x_lo), y: 4, z: 8, core: 2. Of those that a mesh axis runs over, the one named last changes fastest.
Arguments:
- phase: float32 [64, 1024, 512], P('gz', 'gy', 'gx'), may hold values from -1 to 1
- solute: float32 [64, 1024, 512], P('gz', 'gy', 'gx'), may hold values from -1 to 0.5
- advance: int32 [1], replicated, may hold values from 1 to 8
Outputs:
- phase_out: float32 [64, 1024, 512], P('gz', 'gy', 'gx')
- solute_out: float32 [64, 1024, 512], P('gz', 'gy', 'gx')
All inputs are finite; a program needn't handle non-finite values.
Results may differ from a plain program's by a relative error of at most 0.00002.
Values sent between devices are 32-bit elements; how exact they have to be, the bound alone decides.
No kernel may reach another device: no remote copies, remote signals or barrier semaphores. Data moves between devices by JAX's collectives and lax.ppermute only.
A program may use at most 64 MiB of HBM per device.

v0:
```python
import jax
import jax.numpy as jnp
from jax import lax
from jax.sharding import PartitionSpec as P

E_ANI = 0.05
FLOOR = 0.5
LAM = 1.6
DT = 0.1
DSOL = 0.5
KPART = 0.15
GTH = 2.0


def extended(cells, sides, width):
    for axis, dim in sides:
        count = lax.axis_size(axis)
        ends = count - 1
        head = lax.slice_in_dim(cells, 0, width, axis=dim)
        tail = lax.slice_in_dim(cells, cells.shape[dim] - width, cells.shape[dim], axis=dim)
        cells = jnp.concatenate(
            [
                lax.ppermute(tail, axis, [(i, (i + 1) % count) for i in range(ends)]),
                cells,
                lax.ppermute(head, axis, [((i + 1) % count, i) for i in range(ends)]),
            ],
            axis=dim,
        )
    return cells


def shifted(value, axis, steps):
    count = lax.axis_size(axis)
    first, last = (max(0, -steps), min(count, count - steps))
    return lax.ppermute(value, axis, [(source, source + steps) for source in range(first, last)])


def neighbours(ext):
    return [
        ext[2:, 1:-1, 1:-1],
        ext[:-2, 1:-1, 1:-1],
        ext[1:-1, 2:, 1:-1],
        ext[1:-1, :-2, 1:-1],
        ext[1:-1, 1:-1, 2:],
        ext[1:-1, 1:-1, :-2],
    ]


def anisotropy(ext):
    grad_z = (ext[2:, 1:-1, 1:-1] - ext[:-2, 1:-1, 1:-1]) * 0.5
    grad_y = (ext[1:-1, 2:, 1:-1] - ext[1:-1, :-2, 1:-1]) * 0.5
    grad_x = (ext[1:-1, 1:-1, 2:] - ext[1:-1, 1:-1, :-2]) * 0.5
    sq_z, sq_y, sq_x = (grad_z * grad_z, grad_y * grad_y, grad_x * grad_x)
    square = sq_z + sq_y + sq_x
    floor = jnp.maximum(square, FLOOR)
    ratio = (sq_z * sq_z + sq_y * sq_y + sq_x * sq_x) / (floor * floor)
    factor = 1.0 - 3.0 * E_ANI + 4.0 * E_ANI * ratio
    return factor * factor


def divergence(field_ext, coef_ext):
    centre_f = field_ext[1:-1, 1:-1, 1:-1]
    centre_c = coef_ext[1:-1, 1:-1, 1:-1]
    total = jnp.zeros_like(centre_f)
    for near_f, near_c in zip(neighbours(field_ext), neighbours(coef_ext)):
        total = total + 0.5 * (centre_c + near_c) * (near_f - centre_f)
    return total


def boundary_flags():
    return (
        (lax.axis_index("gz") == 0, lax.axis_index("gz") == lax.axis_size("gz") - 1),
        (lax.axis_index("gy") == 0, lax.axis_index("gy") == lax.axis_size("gy") - 1),
        (lax.axis_index("gx") == 0, lax.axis_index("gx") == lax.axis_size("gx") - 1),
    )


def edge_dim(ext, width, dim, at_low, at_high):
    length = ext.shape[dim]
    low_edge = lax.slice_in_dim(ext, width, width + 1, axis=dim)
    high_edge = lax.slice_in_dim(ext, length - width - 1, length - width, axis=dim)
    low_part = lax.slice_in_dim(ext, 0, width, axis=dim)
    middle = lax.slice_in_dim(ext, width, length - width, axis=dim)
    high_part = lax.slice_in_dim(ext, length - width, length, axis=dim)
    low_part = jnp.where(at_low, jnp.repeat(low_edge, width, axis=dim), low_part)
    high_part = jnp.where(at_high, jnp.repeat(high_edge, width, axis=dim), high_part)
    return jnp.concatenate([low_part, middle, high_part], axis=dim)


def edge_all(ext, width, first, flags):
    for offset in range(3):
        ext = edge_dim(ext, width, first + offset, flags[offset][0], flags[offset][1])
    return ext


def thermal_planes(depth, margin):
    total_depth = depth * lax.axis_size("gz")
    planes = (
        lax.axis_index("gz") * depth - margin + jnp.arange(depth + 2 * margin, dtype=jnp.int32)
    ).astype(jnp.float32)
    return (GTH * (planes + 0.5 - total_depth / 2.0) / total_depth)[:, None, None]


def body(phase, solute, advance):
    flags = boundary_flags()
    depth = phase.shape[0]
    total_depth = depth * lax.axis_size("gz")
    phase_ext = extended(phase, (("gz", 0), ("gy", 1), ("gx", 2)), 1)
    phase_ext = edge_all(phase_ext, 1, 0, flags)
    aniso = anisotropy(phase_ext)
    aniso_ext = extended(aniso, (("gz", 0), ("gy", 1), ("gx", 2)), 1)
    aniso_ext = edge_all(aniso_ext, 1, 0, flags)
    lap = divergence(phase_ext, aniso_ext)
    thermal = thermal_planes(depth, 0)
    force = (
        lap + phase - phase * phase * phase - LAM * (1.0 - phase * phase) ** 2 * (solute + thermal)
    )
    phase_new = jnp.clip(phase + DT * force / aniso, -1.0, 1.0)
    rate = (phase_new - phase) / DT
    stacked = jnp.stack([phase_new, solute])
    both_ext = extended(stacked, (("gz", 1), ("gy", 2), ("gx", 3)), 1)
    both_ext = edge_all(both_ext, 1, 1, flags)
    mobility = DSOL * 0.5 * (1.0 - both_ext[0])
    den = 0.5 * (1.0 + KPART) - 0.5 * (1.0 - KPART) * phase_new
    change = divergence(both_ext[1], mobility) + 0.5 * (1.0 + (1.0 - KPART) * solute) * rate
    middle_solute = solute + 0.5 * DT * change / den
    solute_ext = extended(middle_solute, (("gz", 0), ("gy", 1), ("gx", 2)), 1)
    solute_ext = edge_all(solute_ext, 1, 0, flags)
    change = divergence(solute_ext, mobility) + 0.5 * (1.0 + (1.0 - KPART) * middle_solute) * rate
    final_solute = middle_solute + 0.5 * DT * change / den
    fields = jnp.stack([phase_new, final_solute])
    upper = shifted(fields, "gz", -1)
    joined = jnp.concatenate([fields, upper], axis=1)
    shift = advance[0]
    moved = lax.dynamic_slice_in_dim(joined, shift, depth, 1)
    source_plane = lax.axis_index("gz") * depth + jnp.arange(depth, dtype=jnp.int32) + shift
    outside = (source_plane >= total_depth)[:, None, None]
    phase_out = jnp.where(outside, -1.0, moved[0])
    solute_out = jnp.where(outside, 0.0, moved[1])
    return (phase_out, solute_out)


def solution(mesh):
    in_specs = (P("gz", "gy", "gx"), P("gz", "gy", "gx"), P())
    out_specs = (P("gz", "gy", "gx"), P("gz", "gy", "gx"))
    return jax.shard_map(body, mesh=mesh, in_specs=in_specs, out_specs=out_specs, check_vma=False)
```

profile of v0, /device:TPU:69, one launch (start us, length us, event | category | flops | bytes accessed | tf_op | source)
XLA Modules:
  0.0 197.7 jit_solution(8183587871495651094)
XLA Ops:
  1.5 3.1 %collective-permute-start = (f32[1,128,128]{2,1,0:T(8,128)S(1)}, f32[1,128,128]{2,1,0:T(8,128)S(1)}, u32[]{:S(2)}, u32[]{:S(2)}) collective-permute-start(f32[1,128,128]{2,1,0:T(8,128)S(1)} %get-tuple-element.49), channel_id=1, source_target_pairs={{0,32},{32,64},{64,96},{96,128},{128,160},{160,192},{192,224},{1,3... | collective-permute-start | bytes 196616 | tf_op jit(solution)/shard_map/ppermute | solution.py:23
  4.7 3.6 %collective-permute-start.1 = (f32[1,128,128]{2,1,0:T(8,128)S(1)}, f32[1,128,128]{2,1,0:T(8,128)S(1)}, u32[]{:S(2)}, u32[]{:S(2)}) collective-permute-start(f32[1,128,128]{2,1,0:T(8,128)S(1)} %get-tuple-element.48), channel_id=1, source_target_pairs={{32,0},{64,32},{96,64},{128,96},{160,128},{192,160},{224,192},{33,... | collective-permute-start | bytes 196616 | tf_op jit(solution)/shard_map/ppermute | solution.py:25
  9.4 2.7 %collective-permute-done.1 = f32[1,128,128]{2,1,0:T(8,128)S(1)} collective-permute-done((f32[1,128,128]{2,1,0:T(8,128)S(1)}, f32[1,128,128]{2,1,0:T(8,128)S(1)}, u32[]{:S(2)}, u32[]{:S(2)}) %collective-permute-start.1) | collective-permute-done | bytes 65568 | tf_op jit(solution)/shard_map/ppermute | solution.py:25
  12.1 3.5 %collective-permute-start.2 = (f32[10,1,128]{2,1,0:T(1,128)S(1)}, f32[10,1,128]{2,1,0:T(1,128)S(1)}, u32[]{:S(2)}, u32[]{:S(2)}) collective-permute-start(f32[10,1,128]{2,1,0:T(1,128)S(1)} %get-tuple-element.42), channel_id=1, source_target_pairs={{0,4},{4,8},{8,12},{12,16},{16,20},{20,24},{24,28},{1,5},{5,9},{9,... | collective-permute-start | bytes 15368 | tf_op jit(solution)/shard_map/ppermute | solution.py:23
  17.6 3.8 %collective-permute-done.3 = f32[10,1,128]{2,1,0:T(1,128)S(1)} collective-permute-done((f32[10,1,128]{2,1,0:T(1,128)S(1)}, f32[10,1,128]{2,1,0:T(1,128)S(1)}, u32[]{:S(2)}, u32[]{:S(2)}) %collective-permute-start.3) | collective-permute-done | bytes 5152 | tf_op jit(solution)/shard_map/ppermute | solution.py:25
  22.1 6.9 %collective-permute-start.4 = (f32[10,130,1]{1,2,0:T(1,128)S(1)}, f32[10,130,1]{1,2,0:T(1,128)S(1)}, u32[]{:S(2)}, u32[]{:S(2)}) collective-permute-start(f32[10,130,1]{1,2,0:T(1,128)S(1)} %copy.30), channel_id=1, source_target_pairs={{0,1},{1,2},{2,3},{4,5},{5,6},{6,7},{8,9},{9,10},{10,11},{12,13},{... | collective-permute-start | bytes 15608 | tf_op jit(solution)/shard_map/ppermute | solution.py:23
  31.7 2.7 %collective-permute-done.5 = f32[10,130,1]{1,2,0:T(1,128)S(1)} collective-permute-done((f32[10,130,1]{1,2,0:T(1,128)S(1)}, f32[10,130,1]{1,2,0:T(1,128)S(1)}, u32[]{:S(2)}, u32[]{:S(2)}) %collective-permute-start.5) | collective-permute-done | bytes 5232 | tf_op jit(solution)/shard_map/ppermute | solution.py:25
  41.8 4.5 %collective-permute-start.7 = (f32[1,128,128]{2,1,0:T(8,128)S(1)}, f32[1,128,128]{2,1,0:T(8,128)S(1)}, u32[]{:S(2)}, u32[]{:S(2)}) collective-permute-start(f32[1,128,128]{2,1,0:T(8,128)S(1)} %get-tuple-element.47), channel_id=1, source_target_pairs={{32,0},{64,32},{96,64},{128,96},{160,128},{192,160},{224,192},{33,... | collective-permute-start | bytes 196616 | tf_op jit(solution)/shard_map/ppermute | solution.py:25
  46.4 2.9 %collective-permute-done.7 = f32[1,128,128]{2,1,0:T(8,128)S(1)} collective-permute-done((f32[1,128,128]{2,1,0:T(8,128)S(1)}, f32[1,128,128]{2,1,0:T(8,128)S(1)}, u32[]{:S(2)}, u32[]{:S(2)}) %collective-permute-start.7) | collective-permute-done | bytes 65568 | tf_op jit(solution)/shard_map/ppermute | solution.py:25
  49.2 4.9 %collective-permute-start.8 = (f32[10,1,128]{2,1,0:T(1,128)S(1)}, f32[10,1,128]{2,1,0:T(1,128)S(1)}, u32[]{:S(2)}, u32[]{:S(2)}) collective-permute-start(f32[10,1,128]{2,1,0:T(1,128)S(1)} %get-tuple-element.40), channel_id=1, source_target_pairs={{0,4},{4,8},{8,12},{12,16},{16,20},{20,24},{24,28},{1,5},{5,9},{9,... | collective-permute-start | bytes 15368 | tf_op jit(solution)/shard_map/ppermute | solution.py:23
  61.3 5.4 %collective-permute-start.10 = (f32[10,130,1]{1,2,0:T(1,128)S(1)}, f32[10,130,1]{1,2,0:T(1,128)S(1)}, u32[]{:S(2)}, u32[]{:S(2)}) collective-permute-start(f32[10,130,1]{1,2,0:T(1,128)S(1)} %copy.34), channel_id=1, source_target_pairs={{0,1},{1,2},{2,3},{4,5},{5,6},{6,7},{8,9},{9,10},{10,11},{12,13},{... | collective-permute-start | bytes 15608 | tf_op jit(solution)/shard_map/ppermute | solution.py:23
  80.5 4.2 %fusion.9 = f32[8,128,128]{2,1,0:T(8,128)S(1)} fusion(f32[8,128,128]{2,1,0:T(8,128)S(1)} %copy-done.7, f32[10,130,128]{2,1,0:T(8,128)S(1)} %slice.576, f32[10,130,1]{2,1,0:T(8,128)S(1)} %get-tuple-element.19, f32[10,130,1]{2,1,0:T(8,128)S(1)} %get-tuple-element.18, f32[10,128,130]{2,1,0:T(8,128)S(1)} %slice.575, f32[10,1,130]{2,1,0:T(1,128)S(1)} %get-tuple-element.20, ...), kind=kLoop, calls=%fused_computation.44 | loop fusion | flops 10092544 | bytes 5628896 | tf_op jit(solution)/shard_map/jit(clip)/min | solution.py:118
  84.7 3.4 %collective-permute-start.12 = (f32[2,1,128,128]{3,2,1,0:T(8,128)S(1)}, f32[2,1,128,128]{3,2,1,0:T(8,128)S(1)}, u32[]{:S(2)}, u32[]{:S(2)}) collective-permute-start(f32[2,1,128,128]{3,2,1,0:T(8,128)S(1)} %get-tuple-element.30), channel_id=1, source_target_pairs={{0,32},{32,64},{64,96},{96,128},{128,160},{160,192},{192,224},{1,3... | collective-permute-start | bytes 393224 | tf_op jit(solution)/shard_map/ppermute | solution.py:23
  88.2 3.3 %collective-permute-start.13 = (f32[2,1,128,128]{3,2,1,0:T(8,128)S(1)}, f32[2,1,128,128]{3,2,1,0:T(8,128)S(1)}, u32[]{:S(2)}, u32[]{:S(2)}) collective-permute-start(f32[2,1,128,128]{3,2,1,0:T(8,128)S(1)} %get-tuple-element.31), channel_id=1, source_target_pairs={{32,0},{64,32},{96,64},{128,96},{160,128},{192,160},{224,192},{33,... | collective-permute-start | bytes 393224 | tf_op jit(solution)/shard_map/ppermute | solution.py:25
  92.0 4.6 %collective-permute-done.13 = f32[2,1,128,128]{3,2,1,0:T(8,128)S(1)} collective-permute-done((f32[2,1,128,128]{3,2,1,0:T(8,128)S(1)}, f32[2,1,128,128]{3,2,1,0:T(8,128)S(1)}, u32[]{:S(2)}, u32[]{:S(2)}) %collective-permute-start.13) | collective-permute-done | bytes 131104 | tf_op jit(solution)/shard_map/ppermute | solution.py:25
  96.6 2.9 %collective-permute-start.14 = (f32[2,10,1,128]{3,0,2,1:T(2,128)S(1)}, f32[2,10,1,128]{3,0,2,1:T(2,128)S(1)}, u32[]{:S(2)}, u32[]{:S(2)}) collective-permute-start(f32[2,10,1,128]{3,0,2,1:T(2,128)S(1)} %copy.38), channel_id=1, source_target_pairs={{0,4},{4,8},{8,12},{12,16},{16,20},{20,24},{24,28},{1,5},{5,9},{9,... | collective-permute-start | bytes 30728 | tf_op jit(solution)/shard_map/ppermute | solution.py:23
  107.7 5.2 %collective-permute-start.16 = (f32[2,10,130,1]{2,0,3,1:T(2,128)S(1)}, f32[2,10,130,1]{2,0,3,1:T(2,128)S(1)}, u32[]{:S(2)}, u32[]{:S(2)}) collective-permute-start(f32[2,10,130,1]{2,0,3,1:T(2,128)S(1)} %copy.42), channel_id=1, source_target_pairs={{0,1},{1,2},{2,3},{4,5},{5,6},{6,7},{8,9},{9,10},{10,11},{12,13},{... | collective-permute-start | bytes 31208 | tf_op jit(solution)/shard_map/ppermute | solution.py:23
  120.5 2.6 %pad_maximum_fusion = f32[2,10,130,130]{3,2,1,0:T(8,128)S(1)} fusion(f32[2,10,130,1]{3,2,1,0:T(8,128)} %copy.45, f32[2,10,1,128]{3,2,1,0:T(1,128)S(1)} %copy.41, f32[2,1,128,128]{3,2,1,0:T(8,128)S(1)} %collective-permute-done.13, f32[1,8,128,128]{3,2,1,0:T(8,128)S(1)} %bitcast.30, f32[1,8,128,128]{3,2,1,0:T(8,128)S(1)} %bitcast.24, ...), kind=kLoop, calls=%fused_computation | loop fusion | flops 2366000 | bytes 2704000 | tf_op jit(solution)/shard_map/concatenate | solution.py:21
  130.9 4.5 %collective-permute-start.19 = (f32[1,128,128]{2,1,0:T(8,128)S(1)}, f32[1,128,128]{2,1,0:T(8,128)S(1)}, u32[]{:S(2)}, u32[]{:S(2)}) collective-permute-start(f32[1,128,128]{2,1,0:T(8,128)S(1)} %get-tuple-element.45), channel_id=1, source_target_pairs={{32,0},{64,32},{96,64},{128,96},{160,128},{192,160},{224,192},{33,... | collective-permute-start | bytes 196616 | tf_op jit(solution)/shard_map/ppermute | solution.py:25
  135.4 2.9 %collective-permute-done.19 = f32[1,128,128]{2,1,0:T(8,128)S(1)} collective-permute-done((f32[1,128,128]{2,1,0:T(8,128)S(1)}, f32[1,128,128]{2,1,0:T(8,128)S(1)}, u32[]{:S(2)}, u32[]{:S(2)}) %collective-permute-start.19) | collective-permute-done | bytes 65568 | tf_op jit(solution)/shard_map/ppermute | solution.py:25
  138.3 2.9 %collective-permute-start.20 = (f32[10,1,128]{2,1,0:T(1,128)S(1)}, f32[10,1,128]{2,1,0:T(1,128)S(1)}, u32[]{:S(2)}, u32[]{:S(2)}) collective-permute-start(f32[10,1,128]{2,1,0:T(1,128)S(1)} %get-tuple-element.38), channel_id=1, source_target_pairs={{0,4},{4,8},{8,12},{12,16},{16,20},{20,24},{24,28},{1,5},{5,9},{9,... | collective-permute-start | bytes 15368 | tf_op jit(solution)/shard_map/ppermute | solution.py:23
  148.2 5.4 %collective-permute-start.22 = (f32[10,130,1]{1,2,0:T(1,128)S(1)}, f32[10,130,1]{1,2,0:T(1,128)S(1)}, u32[]{:S(2)}, u32[]{:S(2)}) collective-permute-start(f32[10,130,1]{1,2,0:T(1,128)S(1)} %copy.46), channel_id=1, source_target_pairs={{0,1},{1,2},{2,3},{4,5},{5,6},{6,7},{8,9},{9,10},{10,11},{12,13},{... | collective-permute-start | bytes 15608 | tf_op jit(solution)/shard_map/ppermute | solution.py:23
  156.2 2.8 %collective-permute-done.23 = f32[10,130,1]{1,2,0:T(1,128)S(1)} collective-permute-done((f32[10,130,1]{1,2,0:T(1,128)S(1)}, f32[10,130,1]{1,2,0:T(1,128)S(1)}, u32[]{:S(2)}, u32[]{:S(2)}) %collective-permute-start.23) | collective-permute-done | bytes 5232 | tf_op jit(solution)/shard_map/ppermute | solution.py:25
  170.5 24.7 %collective-permute-done.24 = f32[2,8,128,128]{3,2,1,0:T(8,128)} collective-permute-done((f32[2,8,128,128]{3,2,1,0:T(8,128)S(1)}, f32[2,8,128,128]{3,2,1,0:T(8,128)}, u32[]{:S(2)}, u32[]{:S(2)}) %collective-permute-start.24) | collective-permute-done | bytes 1048608 | tf_op jit(solution)/shard_map/ppermute | solution.py:35
  (153 shorter events, 82.1 us)
Async XLA Ops:
  1.5 6.8 %collective-permute-start = (f32[1,128,128]{2,1,0:T(8,128)S(1)}, f32[1,128,128]{2,1,0:T(8,128)S(1)}, u32[]{:S(2)}, u32[]{:S(2)}) collective-permute-start(f32[1,128,128]{2,1,0:T(8,128)S(1)} %get-tuple-element.49), channel_id=1, source_target_pairs={{0,32},{32,64},{64,96},{96,128},{128,160},{160,192},{192,224},{1,3... | collective-permute-start | bytes 196616 | tf_op jit(solution)/shard_map/ppermute | solution.py:23
  4.7 7.4 %collective-permute-start.1 = (f32[1,128,128]{2,1,0:T(8,128)S(1)}, f32[1,128,128]{2,1,0:T(8,128)S(1)}, u32[]{:S(2)}, u32[]{:S(2)}) collective-permute-start(f32[1,128,128]{2,1,0:T(8,128)S(1)} %get-tuple-element.48), channel_id=1, source_target_pairs={{32,0},{64,32},{96,64},{128,96},{160,128},{192,160},{224,192},{33,... | collective-permute-start | bytes 196616 | tf_op jit(solution)/shard_map/ppermute | solution.py:25
  12.1 5.5 %collective-permute-start.2 = (f32[10,1,128]{2,1,0:T(1,128)S(1)}, f32[10,1,128]{2,1,0:T(1,128)S(1)}, u32[]{:S(2)}, u32[]{:S(2)}) collective-permute-start(f32[10,1,128]{2,1,0:T(1,128)S(1)} %get-tuple-element.42), channel_id=1, source_target_pairs={{0,4},{4,8},{8,12},{12,16},{16,20},{20,24},{24,28},{1,5},{5,9},{9,... | collective-permute-start | bytes 15368 | tf_op jit(solution)/shard_map/ppermute | solution.py:23
  15.7 5.8 %collective-permute-start.3 = (f32[10,1,128]{2,1,0:T(1,128)S(1)}, f32[10,1,128]{2,1,0:T(1,128)S(1)}, u32[]{:S(2)}, u32[]{:S(2)}) collective-permute-start(f32[10,1,128]{2,1,0:T(1,128)S(1)} %get-tuple-element.43), channel_id=1, source_target_pairs={{4,0},{8,4},{12,8},{16,12},{20,16},{24,20},{28,24},{5,1},{9,5},{13... | collective-permute-start | bytes 15368 | tf_op jit(solution)/shard_map/ppermute | solution.py:25
  22.1 9.2 %collective-permute-start.4 = (f32[10,130,1]{1,2,0:T(1,128)S(1)}, f32[10,130,1]{1,2,0:T(1,128)S(1)}, u32[]{:S(2)}, u32[]{:S(2)}) collective-permute-start(f32[10,130,1]{1,2,0:T(1,128)S(1)} %copy.30), channel_id=1, source_target_pairs={{0,1},{1,2},{2,3},{4,5},{5,6},{6,7},{8,9},{9,10},{10,11},{12,13},{... | collective-permute-start | bytes 15608 | tf_op jit(solution)/shard_map/ppermute | solution.py:23
  29.4 5.0 %collective-permute-start.5 = (f32[10,130,1]{1,2,0:T(1,128)S(1)}, f32[10,130,1]{1,2,0:T(1,128)S(1)}, u32[]{:S(2)}, u32[]{:S(2)}) collective-permute-start(f32[10,130,1]{1,2,0:T(1,128)S(1)} %copy.31), channel_id=1, source_target_pairs={{1,0},{2,1},{3,2},{5,4},{6,5},{7,6},{9,8},{10,9},{11,10},{13,12},{... | collective-permute-start | bytes 15608 | tf_op jit(solution)/shard_map/ppermute | solution.py:25
  39.6 6.8 %collective-permute-start.6 = (f32[1,128,128]{2,1,0:T(8,128)S(1)}, f32[1,128,128]{2,1,0:T(8,128)S(1)}, u32[]{:S(2)}, u32[]{:S(2)}) collective-permute-start(f32[1,128,128]{2,1,0:T(8,128)S(1)} %get-tuple-element.46), channel_id=1, source_target_pairs={{0,32},{32,64},{64,96},{96,128},{128,160},{160,192},{192,224},{1,3... | collective-permute-start | bytes 196616 | tf_op jit(solution)/shard_map/ppermute | solution.py:23
  41.8 7.4 %collective-permute-start.7 = (f32[1,128,128]{2,1,0:T(8,128)S(1)}, f32[1,128,128]{2,1,0:T(8,128)S(1)}, u32[]{:S(2)}, u32[]{:S(2)}) collective-permute-start(f32[1,128,128]{2,1,0:T(8,128)S(1)} %get-tuple-element.47), channel_id=1, source_target_pairs={{32,0},{64,32},{96,64},{128,96},{160,128},{192,160},{224,192},{33,... | collective-permute-start | bytes 196616 | tf_op jit(solution)/shard_map/ppermute | solution.py:25
  49.2 6.8 %collective-permute-start.8 = (f32[10,1,128]{2,1,0:T(1,128)S(1)}, f32[10,1,128]{2,1,0:T(1,128)S(1)}, u32[]{:S(2)}, u32[]{:S(2)}) collective-permute-start(f32[10,1,128]{2,1,0:T(1,128)S(1)} %get-tuple-element.40), channel_id=1, source_target_pairs={{0,4},{4,8},{8,12},{12,16},{16,20},{20,24},{24,28},{1,5},{5,9},{9,... | collective-permute-start | bytes 15368 | tf_op jit(solution)/shard_map/ppermute | solution.py:23
  54.1 4.4 %collective-permute-start.9 = (f32[10,1,128]{2,1,0:T(1,128)S(1)}, f32[10,1,128]{2,1,0:T(1,128)S(1)}, u32[]{:S(2)}, u32[]{:S(2)}) collective-permute-start(f32[10,1,128]{2,1,0:T(1,128)S(1)} %get-tuple-element.41), channel_id=1, source_target_pairs={{4,0},{8,4},{12,8},{16,12},{20,16},{24,20},{28,24},{5,1},{9,5},{13... | collective-permute-start | bytes 15368 | tf_op jit(solution)/shard_map/ppermute | solution.py:25
  61.3 8.9 %collective-permute-start.10 = (f32[10,130,1]{1,2,0:T(1,128)S(1)}, f32[10,130,1]{1,2,0:T(1,128)S(1)}, u32[]{:S(2)}, u32[]{:S(2)}) collective-permute-start(f32[10,130,1]{1,2,0:T(1,128)S(1)} %copy.34), channel_id=1, source_target_pairs={{0,1},{1,2},{2,3},{4,5},{5,6},{6,7},{8,9},{9,10},{10,11},{12,13},{... | collective-permute-start | bytes 15608 | tf_op jit(solution)/shard_map/ppermute | solution.py:23
  68.2 5.0 %collective-permute-start.11 = (f32[10,130,1]{1,2,0:T(1,128)S(1)}, f32[10,130,1]{1,2,0:T(1,128)S(1)}, u32[]{:S(2)}, u32[]{:S(2)}) collective-permute-start(f32[10,130,1]{1,2,0:T(1,128)S(1)} %copy.35), channel_id=1, source_target_pairs={{1,0},{2,1},{3,2},{5,4},{6,5},{7,6},{9,8},{10,9},{11,10},{13,12},{... | collective-permute-start | bytes 15608 | tf_op jit(solution)/shard_map/ppermute | solution.py:25
  84.7 7.2 %collective-permute-start.12 = (f32[2,1,128,128]{3,2,1,0:T(8,128)S(1)}, f32[2,1,128,128]{3,2,1,0:T(8,128)S(1)}, u32[]{:S(2)}, u32[]{:S(2)}) collective-permute-start(f32[2,1,128,128]{3,2,1,0:T(8,128)S(1)} %get-tuple-element.30), channel_id=1, source_target_pairs={{0,32},{32,64},{64,96},{96,128},{128,160},{160,192},{192,224},{1,3... | collective-permute-start | bytes 393224 | tf_op jit(solution)/shard_map/ppermute | solution.py:23
  88.2 8.3 %collective-permute-start.13 = (f32[2,1,128,128]{3,2,1,0:T(8,128)S(1)}, f32[2,1,128,128]{3,2,1,0:T(8,128)S(1)}, u32[]{:S(2)}, u32[]{:S(2)}) collective-permute-start(f32[2,1,128,128]{3,2,1,0:T(8,128)S(1)} %get-tuple-element.31), channel_id=1, source_target_pairs={{32,0},{64,32},{96,64},{128,96},{160,128},{192,160},{224,192},{33,... | collective-permute-start | bytes 393224 | tf_op jit(solution)/shard_map/ppermute | solution.py:25
  96.6 5.3 %collective-permute-start.14 = (f32[2,10,1,128]{3,0,2,1:T(2,128)S(1)}, f32[2,10,1,128]{3,0,2,1:T(2,128)S(1)}, u32[]{:S(2)}, u32[]{:S(2)}) collective-permute-start(f32[2,10,1,128]{3,0,2,1:T(2,128)S(1)} %copy.38), channel_id=1, source_target_pairs={{0,4},{4,8},{8,12},{12,16},{16,20},{20,24},{24,28},{1,5},{5,9},{9,... | collective-permute-start | bytes 30728 | tf_op jit(solution)/shard_map/ppermute | solution.py:23
  99.5 4.4 %collective-permute-start.15 = (f32[2,10,1,128]{3,0,2,1:T(2,128)S(1)}, f32[2,10,1,128]{3,0,2,1:T(2,128)S(1)}, u32[]{:S(2)}, u32[]{:S(2)}) collective-permute-start(f32[2,10,1,128]{3,0,2,1:T(2,128)S(1)} %copy.39), channel_id=1, source_target_pairs={{4,0},{8,4},{12,8},{16,12},{20,16},{24,20},{28,24},{5,1},{9,5},{13... | collective-permute-start | bytes 30728 | tf_op jit(solution)/shard_map/ppermute | solution.py:25
  107.7 8.2 %collective-permute-start.16 = (f32[2,10,130,1]{2,0,3,1:T(2,128)S(1)}, f32[2,10,130,1]{2,0,3,1:T(2,128)S(1)}, u32[]{:S(2)}, u32[]{:S(2)}) collective-permute-start(f32[2,10,130,1]{2,0,3,1:T(2,128)S(1)} %copy.42), channel_id=1, source_target_pairs={{0,1},{1,2},{2,3},{4,5},{5,6},{6,7},{8,9},{9,10},{10,11},{12,13},{... | collective-permute-start | bytes 31208 | tf_op jit(solution)/shard_map/ppermute | solution.py:23
  113.6 5.2 %collective-permute-start.17 = (f32[2,10,130,1]{2,0,3,1:T(2,128)S(1)}, f32[2,10,130,1]{2,0,3,1:T(2,128)S(1)}, u32[]{:S(2)}, u32[]{:S(2)}) collective-permute-start(f32[2,10,130,1]{2,0,3,1:T(2,128)S(1)} %copy.43), channel_id=1, source_target_pairs={{1,0},{2,1},{3,2},{5,4},{6,5},{7,6},{9,8},{10,9},{11,10},{13,12},{... | collective-permute-start | bytes 31208 | tf_op jit(solution)/shard_map/ppermute | solution.py:25
  128.6 6.8 %collective-permute-start.18 = (f32[1,128,128]{2,1,0:T(8,128)S(1)}, f32[1,128,128]{2,1,0:T(8,128)S(1)}, u32[]{:S(2)}, u32[]{:S(2)}) collective-permute-start(f32[1,128,128]{2,1,0:T(8,128)S(1)} %get-tuple-element.44), channel_id=1, source_target_pairs={{0,32},{32,64},{64,96},{96,128},{128,160},{160,192},{192,224},{1,3... | collective-permute-start | bytes 196616 | tf_op jit(solution)/shard_map/ppermute | solution.py:23
  130.9 7.4 %collective-permute-start.19 = (f32[1,128,128]{2,1,0:T(8,128)S(1)}, f32[1,128,128]{2,1,0:T(8,128)S(1)}, u32[]{:S(2)}, u32[]{:S(2)}) collective-permute-start(f32[1,128,128]{2,1,0:T(8,128)S(1)} %get-tuple-element.45), channel_id=1, source_target_pairs={{32,0},{64,32},{96,64},{128,96},{160,128},{192,160},{224,192},{33,... | collective-permute-start | bytes 196616 | tf_op jit(solution)/shard_map/ppermute | solution.py:25
  138.3 5.3 %collective-permute-start.20 = (f32[10,1,128]{2,1,0:T(1,128)S(1)}, f32[10,1,128]{2,1,0:T(1,128)S(1)}, u32[]{:S(2)}, u32[]{:S(2)}) collective-permute-start(f32[10,1,128]{2,1,0:T(1,128)S(1)} %get-tuple-element.38), channel_id=1, source_target_pairs={{0,4},{4,8},{8,12},{12,16},{16,20},{20,24},{24,28},{1,5},{5,9},{9,... | collective-permute-start | bytes 15368 | tf_op jit(solution)/shard_map/ppermute | solution.py:23
  148.2 7.7 %collective-permute-start.22 = (f32[10,130,1]{1,2,0:T(1,128)S(1)}, f32[10,130,1]{1,2,0:T(1,128)S(1)}, u32[]{:S(2)}, u32[]{:S(2)}) collective-permute-start(f32[10,130,1]{1,2,0:T(1,128)S(1)} %copy.46), channel_id=1, source_target_pairs={{0,1},{1,2},{2,3},{4,5},{5,6},{6,7},{8,9},{9,10},{10,11},{12,13},{... | collective-permute-start | bytes 15608 | tf_op jit(solution)/shard_map/ppermute | solution.py:23
  154.0 5.0 %collective-permute-start.23 = (f32[10,130,1]{1,2,0:T(1,128)S(1)}, f32[10,130,1]{1,2,0:T(1,128)S(1)}, u32[]{:S(2)}, u32[]{:S(2)}) collective-permute-start(f32[10,130,1]{1,2,0:T(1,128)S(1)} %copy.47), channel_id=1, source_target_pairs={{1,0},{2,1},{3,2},{5,4},{6,5},{7,6},{9,8},{10,9},{11,10},{13,12},{... | collective-permute-start | bytes 15608 | tf_op jit(solution)/shard_map/ppermute | solution.py:25
  167.4 27.8 %collective-permute-start.24 = (f32[2,8,128,128]{3,2,1,0:T(8,128)S(1)}, f32[2,8,128,128]{3,2,1,0:T(8,128)}, u32[]{:S(2)}, u32[]{:S(2)}) collective-permute-start(f32[2,8,128,128]{3,2,1,0:T(8,128)S(1)} %pad_maximum_fusion.14), channel_id=1, source_target_pairs={{32,0},{64,32},{96,64},{128,96},{160,128},{192,160},{224,192},{33,... | collective-permute-start | bytes 3145736 | tf_op jit(solution)/shard_map/ppermute | solution.py:35
  (20 other events, 55.6 us)
where the time goes:
time: 201 us; the launch traced here: 198 us
  starting transfers between devices  83.2 us (41%)
  waiting for transfers between devices  58.1 us (29%)
  local copies, waits for them, and re-layouts  29.2 us (15%)
  other arithmetic  24.9 us (12%)
  between operations  2.21 us (1%)
    ppermute x12, starting transfers between devices, extended(): lax.ppermute(tail, axis, [(i, (i + 1) % count) for i in range(ends)])  48 us
    ppermute x12, waiting for transfers between devices, extended(): lax.ppermute(head, axis, [((i + 1) % count, i) for i in range(ends)])  32.9 us
    ppermute x12, starting transfers between devices, extended(): lax.ppermute(head, axis, [((i + 1) % count, i) for i in range(ends)])  32.8 us
    ppermute x1, waiting for transfers between devices, shifted(): lax.ppermute(value, axis, [(source, source + steps) for source in range(f...  24.7 us
    slice x12, local copies, waits for them, and re-layouts, extended(): lax.slice_in_dim(cells, cells.shape[dim] - width, cells.shape[dim], axis=...  9.74 us
    concatenate x8, other arithmetic, extended(): jnp.concatenate([lax.ppermute(tail, axis, [(i, (i + 1) % count) for i in...  7.22 us
    unnamed x40, local copies, waits for them, and re-layouts  6.79 us
    ppermute x5, local copies, waits for them, and re-layouts, extended(): lax.ppermute(head, axis, [((i + 1) % count, i) for i in range(ends)])  4.26 us
  transfers between devices with their start and end apart: 25, of which 14 were waited for; matrix products, arithmetic and copies ran while one was open for 3% of the time, Pallas kernels for 0%

commit v1 on v0

v1 whole, which is shorter than its diff:
```python
import functools

import jax
import jax.numpy as jnp
from jax import lax
from jax.experimental import pallas as pl
from jax.experimental.pallas import tpu as pltpu
from jax.sharding import PartitionSpec as P

E_ANI = 0.05
FLOOR = 0.5
LAM = 1.6
DT = 0.1
DSOL = 0.5
KPART = 0.15
GTH = 2.0

F32 = jnp.float32
DEPTH = 8
ROWS = 160
TILES = 18
VMEM = pl.BlockSpec(memory_space=pltpu.VMEM)
SMEM = pl.BlockSpec(memory_space=pltpu.SMEM)


def lanes():
    return lax.broadcasted_iota(jnp.int32, (8, 128), 1)


def sublanes():
    return lax.broadcasted_iota(jnp.int32, (8, 128), 0)


def swapped(v, step, axis, index):
    size = v.shape[axis]
    return jnp.where((index & step) != 0, pltpu.roll(v, step, axis), pltpu.roll(v, size - step, axis))


def reversed_bits(v, steps, axis, index):
    for step in steps:
        if 2 * step == v.shape[axis]:
            v = pltpu.roll(v, step, axis)
        else:
            v = swapped(v, step, axis, index)
    return v


def reciprocal(v):
    r = pl.reciprocal(v, approx=True)
    return r * (2.0 - v * r)


def pack_kernel(p_ref, u_ref, c_ref, up_ref, down_ref):
    group = lanes() >> 3
    sub = sublanes()
    for t in range(16):
        acc = jnp.zeros((8, 128), F32)
        for f, ref in enumerate((p_ref, u_ref)):
            for z in range(DEPTH):
                v = pltpu.roll(ref[z, 8 * t : 8 * t + 8, :], 64 * f + 8 * z + 4, 1)
                acc = jnp.where(group == 8 * f + z, v, acc)
        c_ref[8 * t : 8 * t + 8, :] = acc
    for z in range(DEPTH):
        up_ref[z] = jnp.where(sub >= 4, p_ref[z, 120:128, :], pltpu.roll(u_ref[z, 120:128, :], 4, 0))
        down_ref[z] = jnp.where(sub < 4, p_ref[z, 0:8, :], pltpu.roll(u_ref[z, 0:8, :], 4, 0))


def strips_kernel(info_ref, c_ref, left_ref, right_ref, up8_ref, down8_ref, s_ref, up_ref, down_ref):
    lane = lanes()
    low = (lane & 4) == 0
    first = info_ref[3] == 0
    last = info_ref[3] == info_ref[6] - 1
    mirror = (low & first) | (jnp.logical_not(low) & last)
    for t in range(16):
        rows = slice(8 * t, 8 * t + 8)
        v = jnp.where(low, left_ref[rows, :], right_ref[rows, :])
        own = reversed_bits(c_ref[rows, :], (1, 2, 4), 1, lane)
        v = jnp.where(mirror, own, v)
        s_ref[rows, :] = v
        if t == 0:
            down_ref[8] = v
        if t == 15:
            up_ref[8] = v
    up_ref[0:8] = up8_ref[...]
    down_ref[0:8] = down8_ref[...]


def halo_kernel(info_ref, from_up_ref, from_down_ref, up_ref, down_ref, s_ref, h_ref):
    sub = sublanes()
    low = sub < 4
    first = info_ref[2] == 0
    last = info_ref[2] == info_ref[5] - 1
    for z in range(9):
        below = jnp.where(first, reversed_bits(down_ref[z], (1, 2, 4), 0, sub), from_up_ref[z])
        above = jnp.where(last, reversed_bits(up_ref[z], (1, 2, 4), 0, sub), from_down_ref[z])
        v = jnp.where(low, above, below)
        if z < 8:
            h_ref[z] = v
            h_ref[8 + z] = pltpu.roll(jnp.where(low, below, above), 4, 0)
        else:
            h_ref[32] = v
    for t in range(16):
        h_ref[16 + t] = s_ref[8 * t : 8 * t + 8, :]


def step_kernel(
    early,
    info_ref,
    p_ref,
    u_ref,
    pn_ref,
    un_ref,
    ex_ref,
    h_ref,
    hn_ref,
    hx_ref,
    phase_ref,
    solute_ref,
    pb,
    ub,
    ab,
    nb,
    db,
    rb,
    sb,
    edges,
    strips,
):
    shift = info_ref[0]
    gz = info_ref[1]
    count_z = info_ref[4]
    total = DEPTH * count_z
    lane = lanes()
    group = lane >> 3
    low = (lane & 4) == 0
    at0 = lane == 0
    at127 = lane == 127
    is_first = gz == 0
    is_last = gz == count_z - 1
    is_second = gz == count_z - 2

    def place(buf, pos, src, index, h, base):
        buf[pos, 16:144, :] = src[index]
        edge = h[base]
        buf[pos, 8:16, :] = edge
        buf[pos, 144:152, :] = edge

    extra_p = 3 if early else 4
    extra_u = 1 if early else 2
    for z in range(DEPTH):
        place(pb, z, p_ref, z, h_ref, z)
        place(ub, z, u_ref, z, h_ref, 8 + z)
    for z in range(pn_ref.shape[0]):
        place(pb, 8 + z, pn_ref, z, hn_ref, z)
    for z in range(un_ref.shape[0]):
        place(ub, 8 + z, un_ref, z, hn_ref, 8 + z)
    for j in range(extra_p):
        pos = 13 + j if early else j
        taken = pos >= 12 + shift if early else pos <= shift - 5

        @pl.when(taken)
        def _():
            place(pb, pos, ex_ref, j, hx_ref, 5 + j if early else j)

    for j in range(extra_u):
        pos = 15 if early else j
        taken = pos >= 14 + shift if early else pos <= shift - 7

        @pl.when(taken)
        def _():
            place(ub, pos, ex_ref, extra_p + j, hx_ref, 8 + (7 if early else j))

    for pos in (12, 13, 14, 15) if early else (0, 1, 2, 3):
        taken = (pos >= 12 + shift) & is_first if early else (pos <= shift - 5) & is_second

        @pl.when(taken)
        def _():
            pb[pos, 8:152, :] = pb[15 - pos, 8:152, :]
            ub[pos, 8:152, :] = ub[15 - pos, 8:152, :]

    @pl.when(is_last)
    def _():
        for pos in (8, 9, 10, 11):
            pb[pos, 8:152, :] = pb[15 - pos, 8:152, :]
            ub[pos, 8:152, :] = ub[15 - pos, 8:152, :]

    fresh = group >= 12 + shift if early else group <= shift - 5
    mirror = (is_last & (group >= 8) & (group < 12)) | (fresh & (is_first if early else is_second))
    for t in range(TILES):
        src = 32 if t in (0, TILES - 1) else 15 + t
        own, near, far = h_ref[src], hn_ref[src], hx_ref[src]
        own_r, near_r, far_r = (pltpu.roll(v, 64, 1) for v in (own, near, far))
        cp = jnp.where(group < 8, own, near_r)
        cu = jnp.where(group < 8, own_r, near)
        cp = jnp.where(fresh, far_r if early else far, cp)
        cu = jnp.where(fresh, far if early else far_r, cu)
        cp = jnp.where(mirror, reversed_bits(cp, (8, 16, 32, 64), 1, lane), cp)
        cu = jnp.where(mirror, reversed_bits(cu, (8, 16, 32, 64), 1, lane), cu)
        rows = slice(8 + 8 * t, 16 + 8 * t)
        edges[0, rows, :] = cp
        edges[1, rows, :] = cu
        gp = jnp.zeros((8, 128), F32)
        gu = jnp.zeros((8, 128), F32)
        for pos in range(16):
            gp = jnp.where(group == pos, pltpu.roll(pb[pos, rows, :], 8 * pos + 4, 1), gp)
            gu = jnp.where(group == pos, pltpu.roll(ub[pos, rows, :], 8 * pos + 4, 1), gu)
        strips[0, 0, rows, :] = jnp.where(low, cp, gp)
        strips[0, 1, rows, :] = jnp.where(low, gp, cp)
        strips[1, 0, rows, :] = jnp.where(low, cu, gu)
        strips[1, 1, rows, :] = jnp.where(low, gu, cu)

    def aniso_of(dz, dy, dx):
        sz, sy, sx = dz * dz, dy * dy, dx * dx
        floor = jnp.maximum(sz + sy + sx, 4.0 * FLOOR)
        ratio = (sz * sz + sy * sy + sx * sx) * reciprocal(floor * floor)
        factor = (1.0 - 3.0 * E_ANI) + (4.0 * E_ANI) * ratio
        return factor * factor

    def flux_sum(f, c, fs, cs):
        acc = None
        for near_f, near_c in zip(fs, cs):
            term = (c + near_c) * (near_f - f)
            acc = term if acc is None else acc + term
        return acc

    def phase_of(p, a, u, total_flux, thermal):
        om = 1.0 - p * p
        force = 0.5 * total_flux + om * (p - LAM * om * (u + thermal))
        new = jnp.clip(p + DT * (force * reciprocal(a)), -1.0, 1.0)
        den = 0.5 * (1.0 + KPART) - 0.5 * (1.0 - KPART) * new
        return 1.0 - new, new - p, 0.125 * DT * DSOL * reciprocal(den)

    def solute_of(u, d, r, total_flux):
        k = 0.5 / DT / (0.25 * DSOL)
        return u + r * (total_flux + (k + k * (1.0 - KPART) * u) * d)

    def thermal_of(g):
        g = jnp.where(g < 0, -1 - g, g)
        g = jnp.where(g >= total, 2 * total - 1 - g, g)
        return (GTH * (g.astype(F32) + 0.5 - total.astype(F32) / 2.0)) / total.astype(F32)

    q_lane = shift - 4 + ((group - (shift - 4)) & 15)
    strip_thermal = thermal_of(DEPTH * gz + q_lane)

    def strip_near(field, side, r0):
        v = strips[field, side, r0 : r0 + 8, :]
        return v, (
            pltpu.roll(v, 120, 1),
            pltpu.roll(v, 8, 1),
            strips[field, side, r0 + 1 : r0 + 9, :],
            strips[field, side, r0 - 1 : r0 + 7, :],
            pltpu.roll(v, 127, 1),
            pltpu.roll(v, 1, 1),
        )

    def strip_stage(fn, edge):
        for t in range(TILES):
            r0 = 8 + 8 * t
            left = fn(0, r0)
            right = fn(1, r0)
            edges[edge, r0 : r0 + 8, :] = jnp.where(low, left, right)

    def strip_aniso(side, r0):
        _, n = strip_near(0, side, r0)
        a = aniso_of(n[0] - n[1], n[2] - n[3], n[4] - n[5])
        strips[2, side, r0 : r0 + 8, :] = a
        return a

    def strip_phase(side, r0):
        p, ps = strip_near(0, side, r0)
        a, as_ = strip_near(2, side, r0)
        u = strips[1, side, r0 : r0 + 8, :]
        n, d, r = phase_of(p, a, u, flux_sum(p, a, ps, as_), strip_thermal)
        strips[3, side, r0 : r0 + 8, :] = n
        strips[4, side, r0 : r0 + 8, :] = d
        strips[5, side, r0 : r0 + 8, :] = r
        return n

    def strip_solute(side, r0):
        u, us = strip_near(1, side, r0)
        n, ns = strip_near(3, side, r0)
        d = strips[4, side, r0 : r0 + 8, :]
        r = strips[5, side, r0 : r0 + 8, :]
        return solute_of(u, d, r, flux_sum(u, n, us, ns))

    strip_stage(strip_aniso, 2)
    strip_stage(strip_phase, 3)
    strip_stage(strip_solute, 4)

    def near(buf, edge, q, r0):
        p = q & 15
        v = buf[p, r0 : r0 + 8, :]
        e = pltpu.roll(edges[edge, r0 : r0 + 8, :], 124 - 8 * p, 1)
        return v, (
            buf[(q + 1) & 15, r0 : r0 + 8, :],
            buf[(q - 1) & 15, r0 : r0 + 8, :],
            buf[p, r0 + 1 : r0 + 9, :],
            buf[p, r0 - 1 : r0 + 7, :],
            pltpu.roll(jnp.where(at0, e, v), 127, 1),
            pltpu.roll(jnp.where(at127, e, v), 1, 1),
        )

    def stage(first, count, tiles, fn):
        def step(i, carry):
            for t in tiles:
                fn(shift + first + i, 8 + 8 * t)
            return carry

        lax.fori_loop(0, count, step, 0)

    def plane_aniso(q, r0):
        _, n = near(pb, 0, q, r0)
        ab[q & 15, r0 : r0 + 8, :] = aniso_of(n[0] - n[1], n[2] - n[3], n[4] - n[5])

    def plane_phase(q, r0):
        p, ps = near(pb, 0, q, r0)
        a, as_ = near(ab, 2, q, r0)
        u = ub[q & 15, r0 : r0 + 8, :]
        n, d, r = phase_of(p, a, u, flux_sum(p, a, ps, as_), thermal_of(DEPTH * gz + q))
        nb[q & 15, r0 : r0 + 8, :] = n
        db[q & 15, r0 : r0 + 8, :] = d
        rb[q & 15, r0 : r0 + 8, :] = r

    def substep(buf, edge, q, r0):
        u, us = near(buf, edge, q, r0)
        n, ns = near(nb, 3, q, r0)
        return n, solute_of(u, db[q & 15, r0 : r0 + 8, :], rb[q & 15, r0 : r0 + 8, :], flux_sum(u, n, us, ns))

    def plane_first(q, r0):
        _, v = substep(ub, 1, q, r0)
        sb[q & 15, r0 : r0 + 8, :] = v

    def plane_second(q, r0):
        n, v = substep(sb, 4, q, r0)
        outside = DEPTH * gz + q >= total
        phase_ref[q - shift, r0 - 16 : r0 - 8, :] = jnp.where(outside, -1.0, 1.0 - n)
        solute_ref[q - shift, r0 - 16 : r0 - 8, :] = jnp.where(outside, 0.0, v)

    every = range(TILES)
    stage(-3, 14, every, plane_aniso)
    stage(-2, 12, every, plane_phase)
    stage(-1, 10, every, plane_first)
    stage(0, 8, range(1, TILES - 1), plane_second)


def moved(value, axis, steps):
    count = lax.axis_size(axis)
    first, last = (max(0, -steps), min(count, count - steps))
    return lax.ppermute(value, axis, [(source, source + steps) for source in range(first, last)])


def out(*shape):
    return jax.ShapeDtypeStruct(shape, F32)


def call(kernel, shapes, n_smem, *args, scratch=()):
    return pl.pallas_call(
        kernel,
        out_shape=shapes,
        in_specs=[SMEM] * n_smem + [VMEM] * (len(args) - n_smem),
        out_specs=jax.tree.map(lambda _: VMEM, shapes),
        scratch_shapes=scratch,
        compiler_params=pltpu.CompilerParams(vmem_limit_bytes=40 * 1024 * 1024),
    )(*args)


def branch(early, phase, solute, info):
    near_p = moved(phase[0:7] if early else phase, "gz", -1)
    near_u = moved(solute[0:5] if early else solute, "gz", -1)
    if early:
        extra = moved(jnp.concatenate([phase[5:8], solute[7:8]]), "gz", 1)
    else:
        extra = moved(jnp.concatenate([phase[0:4], solute[0:2]]), "gz", -2)
    own_c, up8, down8 = call(pack_kernel, (out(128, 128), out(8, 8, 128), out(8, 8, 128)), 0, phase, solute)
    left = moved(own_c, "gx", 1)
    right = moved(own_c, "gx", -1)
    strip, up, down = call(
        strips_kernel, (out(128, 128), out(9, 8, 128), out(9, 8, 128)), 1, info, own_c, left, right, up8, down8
    )
    from_up = moved(up, "gy", 1)
    from_down = moved(down, "gy", -1)
    halo = call(halo_kernel, out(33, 8, 128), 1, info, from_up, from_down, up, down, strip)
    near_h = moved(halo, "gz", -1)
    extra_h = moved(halo, "gz", 1 if early else -2)
    whole = pltpu.VMEM((16, ROWS, 128), F32)
    return call(
        functools.partial(step_kernel, early),
        (out(*phase.shape), out(*phase.shape)),
        1,
        info,
        phase,
        solute,
        near_p,
        near_u,
        extra,
        halo,
        near_h,
        extra_h,
        scratch=[whole] * 7 + [pltpu.VMEM((5, ROWS, 128), F32), pltpu.VMEM((6, 2, ROWS, 128), F32)],
    )


def body(phase, solute, advance):
    axes = ("gz", "gy", "gx")
    info = jnp.stack(
        [advance[0]] + [lax.axis_index(a) for a in axes] + [jnp.int32(lax.axis_size(a)) for a in axes]
    ).astype(jnp.int32)
    return lax.cond(
        advance[0] < 4, functools.partial(branch, True), functools.partial(branch, False), phase, solute, info
    )


def solution(mesh):
    in_specs = (P("gz", "gy", "gx"), P("gz", "gy", "gx"), P())
    out_specs = (P("gz", "gy", "gx"), P("gz", "gy", "gx"))
    return jax.shard_map(body, mesh=mesh, in_specs=in_specs, out_specs=out_specs, check_vma=False)
```

time: 201 us -> 74.5 us (0.37)
  the two profiles are of different devices: /device:TPU:69 before, /device:TPU:122 now
where the time goes in v1:
time: 74.5 us; the launch traced here: 74.2 us
  starting transfers between devices  25.5 us (34%)
  waiting for transfers between devices  23.9 us (32%)
  Pallas kernels  21.2 us (28%)
  local copies, waits for them, and re-layouts  2.08 us (3%)
  between operations  1.29 us (2%)
    ppermute x9, starting transfers between devices, moved(): lax.ppermute(value, axis, [(source, source + steps) for source in range(f...  25.5 us
    ppermute x9, waiting for transfers between devices, moved(): lax.ppermute(value, axis, [(source, source + steps) for source in range(f...  23.9 us
    pallas_call x4, Pallas kernels, call(): pl.pallas_call(kernel, out_shape=shapes, in_specs=[SMEM] * n_smem + [VMEM...  21.2 us
    slice x2, local copies, waits for them, and re-layouts, branch(): extra = moved(jnp.concatenate([phase[0:4], solute[0:2]]), 'gz', -2)  1.98 us
  transfers between devices with their start and end apart: 9, of which 5 were waited for; matrix products, arithmetic and copies ran while one was open for 3% of the time, Pallas kernels for 2%

profile of v1, /device:TPU:122, one launch (start us, length us, event | category | flops | bytes accessed | tf_op | source)
XLA Modules:
  0.0 74.2 jit_solution(5061107022656615711)
XLA Ops:
  1.3 0.1 stack.15
  1.4 72.8 %conditional.1 = ((f32[8,128,128]{2,1,0:T(8,128)}, f32[8,128,128]{2,1,0:T(8,128)})) conditional(s32[]{:T(128)} %bitcast, (f32[8,128,128]{2,1,0:T(8,128)}, f32[8,128,128]{2,1,0:T(8,128)}, s32[7]{0:T(128)S(1)}) %tuple.13, (f32[8,128,128]{2,1,0:T(8,128)}, f32[8,128,128]{2,1,0:T(8,128)}, s32[7]{0:T(128)S(1)}) %tuple.13), branch_computations={%region_0.0_spmd, %region_1.0_spmd} | conditional | flops 98304 | bytes 13435304 | solution.py:408
  1.4 4.2 %collective-permute-start = (f32[8,128,128]{2,1,0:T(8,128)}, f32[8,128,128]{2,1,0:T(8,128)S(1)}, u32[]{:S(2)}, u32[]{:S(2)}) collective-permute-start(f32[8,128,128]{2,1,0:T(8,128)} %get-tuple-element.42.p_ref), channel_id=1, source_target_pairs={{32,0},{64,32},{96,64},{128,96},{160,128},{192,160},{224,192},{33,... | collective-permute-start | bytes 1572872 | tf_op jit(solution)/shard_map/cond/branch_0_fun/ppermute | solution.py:349
  5.6 3.3 %collective-permute-start.1 = (f32[8,128,128]{2,1,0:T(8,128)}, f32[8,128,128]{2,1,0:T(8,128)S(1)}, u32[]{:S(2)}, u32[]{:S(2)}) collective-permute-start(f32[8,128,128]{2,1,0:T(8,128)} %get-tuple-element.44.u_ref), channel_id=1, source_target_pairs={{32,0},{64,32},{96,64},{128,96},{160,128},{192,160},{224,192},{33,... | collective-permute-start | bytes 1572872 | tf_op jit(solution)/shard_map/cond/branch_0_fun/ppermute | solution.py:349
  8.9 0.9 %slice.13 = f32[2,128,128]{2,1,0:T(8,128)S(1)} slice(f32[8,128,128]{2,1,0:T(8,128)} %get-tuple-element.44.u_ref), slice={[0:2], [0:128], [0:128]} | slice | bytes 262144 | tf_op jit(solution)/shard_map/cond/branch_0_fun/slice | solution.py:373
  9.8 0.0 copy-start
  9.9 0.0 copy-start.2
  9.9 1.1 %slice.12 = f32[4,128,128]{2,1,0:T(8,128)S(1)} slice(f32[8,128,128]{2,1,0:T(8,128)} %get-tuple-element.42.p_ref), slice={[0:4], [0:128], [0:128]} | slice | bytes 524288 | tf_op jit(solution)/shard_map/cond/branch_0_fun/slice | solution.py:373
  11.0 2.4 %collective-permute-start.2 = (f32[6,128,128]{2,1,0:T(8,128)S(1)}, f32[6,128,128]{2,1,0:T(8,128)S(1)}, u32[]{:S(2)}, u32[]{:S(2)}) collective-permute-start(f32[6,128,128]{2,1,0:T(8,128)S(1)} %pad_maximum_fusion), channel_id=1, source_target_pairs={{64,0},{96,32},{128,64},{160,96},{192,128},{224,160},{65,1},{97,33... | collective-permute-start | bytes 1179656 | tf_op jit(solution)/shard_map/cond/branch_0_fun/ppermute | solution.py:349
  13.4 0.3 branch_0_fun.4
  13.7 1.9 %collective-permute-start.4 = (f32[128,128]{1,0:T(8,128)S(1)}, f32[128,128]{1,0:T(8,128)S(1)}, u32[]{:S(2)}, u32[]{:S(2)}) collective-permute-start(f32[128,128]{1,0:T(8,128)S(1)} %get-tuple-element.15.c_ref), channel_id=1, source_target_pairs={{1,0},{2,1},{3,2},{5,4},{6,5},{7,6},{9,8},{10,9},{11,10},{13,12},{... | collective-permute-start | bytes 196616 | tf_op jit(solution)/shard_map/cond/branch_0_fun/ppermute | solution.py:349
  15.6 2.4 %collective-permute-start.3 = (f32[128,128]{1,0:T(8,128)S(1)}, f32[128,128]{1,0:T(8,128)S(1)}, u32[]{:S(2)}, u32[]{:S(2)}) collective-permute-start(f32[128,128]{1,0:T(8,128)S(1)} %get-tuple-element.15.c_ref), channel_id=1, source_target_pairs={{0,1},{1,2},{2,3},{4,5},{5,6},{6,7},{8,9},{9,10},{10,11},{12,13},{... | collective-permute-start | bytes 196616 | tf_op jit(solution)/shard_map/cond/branch_0_fun/ppermute | solution.py:349
  18.1 10.9 %collective-permute-done.4.right_ref = f32[128,128]{1,0:T(8,128)S(1)} collective-permute-done((f32[128,128]{1,0:T(8,128)S(1)}, f32[128,128]{1,0:T(8,128)S(1)}, u32[]{:S(2)}, u32[]{:S(2)}) %collective-permute-start.4) | collective-permute-done | bytes 65568 | tf_op jit(solution)/shard_map/cond/branch_0_fun/ppermute | solution.py:349
  28.9 1.4 %collective-permute-done.3.left_ref = f32[128,128]{1,0:T(8,128)S(1)} collective-permute-done((f32[128,128]{1,0:T(8,128)S(1)}, f32[128,128]{1,0:T(8,128)S(1)}, u32[]{:S(2)}, u32[]{:S(2)}) %collective-permute-start.3) | collective-permute-done | bytes 65568 | tf_op jit(solution)/shard_map/cond/branch_0_fun/ppermute | solution.py:349
  30.3 0.8 %branch_0_fun.5 = (f32[128,128]{1,0:T(8,128)S(1)}, f32[9,8,128]{2,1,0:T(8,128)S(1)}, f32[9,8,128]{2,1,0:T(8,128)S(1)}) custom-call(s32[7]{0:T(128)S(1)} %get-tuple-element.12.info_ref, f32[128,128]{1,0:T(8,128)S(1)} %get-tuple-element.15.c_ref, f32[128,128]{1,0:T(8,128)S(1)} %collective-permute-done.3.left_ref, ...), custom_call_target="tpu_custom_call" | custom-call | tf_op jit(solution)/shard_map/cond/branch_0_fun/pallas_call | solution.py:357
  31.1 5.0 %collective-permute-start.5 = (f32[9,8,128]{2,1,0:T(8,128)S(1)}, f32[9,8,128]{2,1,0:T(8,128)S(1)}, u32[]{:S(2)}, u32[]{:S(2)}) collective-permute-start(f32[9,8,128]{2,1,0:T(8,128)S(1)} %get-tuple-element.18.up_ref), channel_id=1, source_target_pairs={{0,4},{4,8},{8,12},{12,16},{16,20},{20,24},{24,28},{1,5},{5,9},{9,... | collective-permute-start | bytes 110600 | tf_op jit(solution)/shard_map/cond/branch_0_fun/ppermute | solution.py:349
  36.2 1.9 %collective-permute-start.6 = (f32[9,8,128]{2,1,0:T(8,128)S(1)}, f32[9,8,128]{2,1,0:T(8,128)S(1)}, u32[]{:S(2)}, u32[]{:S(2)}) collective-permute-start(f32[9,8,128]{2,1,0:T(8,128)S(1)} %get-tuple-element.19.down_ref), channel_id=1, source_target_pairs={{4,0},{8,4},{12,8},{16,12},{20,16},{24,20},{28,24},{5,1},{9,5},{13... | collective-permute-start | bytes 110600 | tf_op jit(solution)/shard_map/cond/branch_0_fun/ppermute | solution.py:349
  38.1 5.1 %collective-permute-done.6.from_down_ref = f32[9,8,128]{2,1,0:T(8,128)S(1)} collective-permute-done((f32[9,8,128]{2,1,0:T(8,128)S(1)}, f32[9,8,128]{2,1,0:T(8,128)S(1)}, u32[]{:S(2)}, u32[]{:S(2)}) %collective-permute-start.6) | collective-permute-done | bytes 36896 | tf_op jit(solution)/shard_map/cond/branch_0_fun/ppermute | solution.py:349
  43.2 0.6 branch_0_fun.6.h_ref
  43.8 2.4 %collective-permute-start.8 = (f32[33,8,128]{2,1,0:T(8,128)S(1)}, f32[33,8,128]{2,1,0:T(8,128)S(1)}, u32[]{:S(2)}, u32[]{:S(2)}) collective-permute-start(f32[33,8,128]{2,1,0:T(8,128)S(1)} %branch_0_fun.6.h_ref), channel_id=1, source_target_pairs={{64,0},{96,32},{128,64},{160,96},{192,128},{224,160},{65,1},{97,33... | collective-permute-start | bytes 405512 | tf_op jit(solution)/shard_map/cond/branch_0_fun/ppermute | solution.py:349
  46.2 1.9 %collective-permute-start.7 = (f32[33,8,128]{2,1,0:T(8,128)S(1)}, f32[33,8,128]{2,1,0:T(8,128)S(1)}, u32[]{:S(2)}, u32[]{:S(2)}) collective-permute-start(f32[33,8,128]{2,1,0:T(8,128)S(1)} %branch_0_fun.6.h_ref), channel_id=1, source_target_pairs={{32,0},{64,32},{96,64},{128,96},{160,128},{192,160},{224,192},{33,... | collective-permute-start | bytes 405512 | tf_op jit(solution)/shard_map/cond/branch_0_fun/ppermute | solution.py:349
  48.1 0.6 collective-permute-done.8.hx_ref
  48.7 5.9 %collective-permute-done.7.hn_ref = f32[33,8,128]{2,1,0:T(8,128)S(1)} collective-permute-done((f32[33,8,128]{2,1,0:T(8,128)S(1)}, f32[33,8,128]{2,1,0:T(8,128)S(1)}, u32[]{:S(2)}, u32[]{:S(2)}) %collective-permute-start.7) | collective-permute-done | bytes 135200 | tf_op jit(solution)/shard_map/cond/branch_0_fun/ppermute | solution.py:349
  54.6 19.6 %branch_0_fun.7 = (f32[8,128,128]{2,1,0:T(8,128)}, f32[8,128,128]{2,1,0:T(8,128)}) custom-call(s32[7]{0:T(128)S(1)} %get-tuple-element.12.info_ref, f32[8,128,128]{2,1,0:T(8,128)S(1)} %copy-done, f32[8,128,128]{2,1,0:T(8,128)S(1)} %copy-done.2, f32[8,128,128]{2,1,0:T(8,128)S(1)} %collective-permute-done.pn_ref, ...), custom_call_target="tpu_custom_call" | custom-call | tf_op jit(solution)/shard_map/cond/branch_0_fun/pallas_call | solution.py:357
  (8 shorter events, 0.0 us)
Async XLA Ops:
  1.4 53.2 %collective-permute-start = (f32[8,128,128]{2,1,0:T(8,128)}, f32[8,128,128]{2,1,0:T(8,128)S(1)}, u32[]{:S(2)}, u32[]{:S(2)}) collective-permute-start(f32[8,128,128]{2,1,0:T(8,128)} %get-tuple-element.42.p_ref), channel_id=1, source_target_pairs={{32,0},{64,32},{96,64},{128,96},{160,128},{192,160},{224,192},{33,... | collective-permute-start | bytes 1572872 | tf_op jit(solution)/shard_map/cond/branch_0_fun/ppermute | solution.py:349
  5.6 49.0 %collective-permute-start.1 = (f32[8,128,128]{2,1,0:T(8,128)}, f32[8,128,128]{2,1,0:T(8,128)S(1)}, u32[]{:S(2)}, u32[]{:S(2)}) collective-permute-start(f32[8,128,128]{2,1,0:T(8,128)} %get-tuple-element.44.u_ref), channel_id=1, source_target_pairs={{32,0},{64,32},{96,64},{128,96},{160,128},{192,160},{224,192},{33,... | collective-permute-start | bytes 1572872 | tf_op jit(solution)/shard_map/cond/branch_0_fun/ppermute | solution.py:349
  9.8 3.5 %copy-start = (f32[8,128,128]{2,1,0:T(8,128)S(1)}, f32[8,128,128]{2,1,0:T(8,128)}, u32[]{:S(2)}) copy-start(f32[8,128,128]{2,1,0:T(8,128)} %get-tuple-element.42.p_ref) | copy-start | bytes 1572868 | tf_op jit(solution)/shard_map/cond
  9.9 3.5 %copy-start.2 = (f32[8,128,128]{2,1,0:T(8,128)S(1)}, f32[8,128,128]{2,1,0:T(8,128)}, u32[]{:S(2)}) copy-start(f32[8,128,128]{2,1,0:T(8,128)} %get-tuple-element.44.u_ref) | copy-start | bytes 1572868 | tf_op jit(solution)/shard_map/cond
  11.0 43.6 %collective-permute-start.2 = (f32[6,128,128]{2,1,0:T(8,128)S(1)}, f32[6,128,128]{2,1,0:T(8,128)S(1)}, u32[]{:S(2)}, u32[]{:S(2)}) collective-permute-start(f32[6,128,128]{2,1,0:T(8,128)S(1)} %pad_maximum_fusion), channel_id=1, source_target_pairs={{64,0},{96,32},{128,64},{160,96},{192,128},{224,160},{65,1},{97,33... | collective-permute-start | bytes 1179656 | tf_op jit(solution)/shard_map/cond/branch_0_fun/ppermute | solution.py:349
  13.7 15.2 %collective-permute-start.4 = (f32[128,128]{1,0:T(8,128)S(1)}, f32[128,128]{1,0:T(8,128)S(1)}, u32[]{:S(2)}, u32[]{:S(2)}) collective-permute-start(f32[128,128]{1,0:T(8,128)S(1)} %get-tuple-element.15.c_ref), channel_id=1, source_target_pairs={{1,0},{2,1},{3,2},{5,4},{6,5},{7,6},{9,8},{10,9},{11,10},{13,12},{... | collective-permute-start | bytes 196616 | tf_op jit(solution)/shard_map/cond/branch_0_fun/ppermute | solution.py:349
  15.6 14.7 %collective-permute-start.3 = (f32[128,128]{1,0:T(8,128)S(1)}, f32[128,128]{1,0:T(8,128)S(1)}, u32[]{:S(2)}, u32[]{:S(2)}) collective-permute-start(f32[128,128]{1,0:T(8,128)S(1)} %get-tuple-element.15.c_ref), channel_id=1, source_target_pairs={{0,1},{1,2},{2,3},{4,5},{5,6},{6,7},{8,9},{9,10},{10,11},{12,13},{... | collective-permute-start | bytes 196616 | tf_op jit(solution)/shard_map/cond/branch_0_fun/ppermute | solution.py:349
  31.1 7.0 %collective-permute-start.5 = (f32[9,8,128]{2,1,0:T(8,128)S(1)}, f32[9,8,128]{2,1,0:T(8,128)S(1)}, u32[]{:S(2)}, u32[]{:S(2)}) collective-permute-start(f32[9,8,128]{2,1,0:T(8,128)S(1)} %get-tuple-element.18.up_ref), channel_id=1, source_target_pairs={{0,4},{4,8},{8,12},{12,16},{16,20},{20,24},{24,28},{1,5},{5,9},{9,... | collective-permute-start | bytes 110600 | tf_op jit(solution)/shard_map/cond/branch_0_fun/ppermute | solution.py:349
  36.2 7.1 %collective-permute-start.6 = (f32[9,8,128]{2,1,0:T(8,128)S(1)}, f32[9,8,128]{2,1,0:T(8,128)S(1)}, u32[]{:S(2)}, u32[]{:S(2)}) collective-permute-start(f32[9,8,128]{2,1,0:T(8,128)S(1)} %get-tuple-element.19.down_ref), channel_id=1, source_target_pairs={{4,0},{8,4},{12,8},{16,12},{20,16},{24,20},{28,24},{5,1},{9,5},{13... | collective-permute-start | bytes 110600 | tf_op jit(solution)/shard_map/cond/branch_0_fun/ppermute | solution.py:349
  43.8 4.9 %collective-permute-start.8 = (f32[33,8,128]{2,1,0:T(8,128)S(1)}, f32[33,8,128]{2,1,0:T(8,128)S(1)}, u32[]{:S(2)}, u32[]{:S(2)}) collective-permute-start(f32[33,8,128]{2,1,0:T(8,128)S(1)} %branch_0_fun.6.h_ref), channel_id=1, source_target_pairs={{64,0},{96,32},{128,64},{160,96},{192,128},{224,160},{65,1},{97,33... | collective-permute-start | bytes 405512 | tf_op jit(solution)/shard_map/cond/branch_0_fun/ppermute | solution.py:349
  46.2 8.4 %collective-permute-start.7 = (f32[33,8,128]{2,1,0:T(8,128)S(1)}, f32[33,8,128]{2,1,0:T(8,128)S(1)}, u32[]{:S(2)}, u32[]{:S(2)}) collective-permute-start(f32[33,8,128]{2,1,0:T(8,128)S(1)} %branch_0_fun.6.h_ref), channel_id=1, source_target_pairs={{32,0},{64,32},{96,64},{128,96},{160,128},{192,160},{224,192},{33,... | collective-permute-start | bytes 405512 | tf_op jit(solution)/shard_map/cond/branch_0_fun/ppermute | solution.py:349

commit v2 on v1

--- a/solution.py
+++ b/solution.py
@@ -123,9 +123,13 @@
     db,
     rb,
     sb,
-    edges,
-    strips,
+    pl_b,
+    pr_b,
+    nl_b,
+    nr_b,
+    *more,
 ):
+    edges, strips = more[:5], more[5:]
     shift = info_ref[0]
     gz = info_ref[1]
     count_z = info_ref[4]
@@ -192,22 +196,42 @@
         own_r, near_r, far_r = (pltpu.roll(v, 64, 1) for v in (own, near, far))
         cp = jnp.where(group < 8, own, near_r)
         cu = jnp.where(group < 8, own_r, near)
-        cp = jnp.where(fresh, far_r if early else far, cp)
-        cu = jnp.where(fresh, far if early else far_r, cu)
-        cp = jnp.where(mirror, reversed_bits(cp, (8, 16, 32, 64), 1, lane), cp)
-        cu = jnp.where(mirror, reversed_bits(cu, (8, 16, 32, 64), 1, lane), cu)
         rows = slice(8 + 8 * t, 16 + 8 * t)
-        edges[0, rows, :] = cp
-        edges[1, rows, :] = cu
+        edges[0][rows, :] = jnp.where(fresh, far_r if early else far, cp)
+        edges[1][rows, :] = jnp.where(fresh, far if early else far_r, cu)
+
+    @pl.when(is_last | (is_first if early else is_second))
+    def _():
+        back = is_first if early else False
+        pick = (lane >> 3) & 3
+        for t in range(TILES):
+            rows = slice(8 + 8 * t, 16 + 8 * t)
+            for field in (0, 1):
+                v = edges[field][rows, :]
+                m = v
+                for j in range(4):
+                    amount = 8 * (2 * j + 1)
+                    if early:
+                        turned = pltpu.roll(v, jnp.where(back, 128 - amount, amount), 1)
+                        m = jnp.where(pick == jnp.where(back, 3 - j, j), turned, m)
+                    else:
+                        m = jnp.where(pick == j, pltpu.roll(v, amount, 1), m)
+                edges[field][rows, :] = jnp.where(mirror, m, v)
+
+    for t in range(TILES):
+        rows = slice(8 + 8 * t, 16 + 8 * t)
+        cp = edges[0][rows, :]
+        cu = edges[1][rows, :]
         gp = jnp.zeros((8, 128), F32)
         gu = jnp.zeros((8, 128), F32)
         for pos in range(16):
             gp = jnp.where(group == pos, pltpu.roll(pb[pos, rows, :], 8 * pos + 4, 1), gp)
+        for pos in range(16):
             gu = jnp.where(group == pos, pltpu.roll(ub[pos, rows, :], 8 * pos + 4, 1), gu)
-        strips[0, 0, rows, :] = jnp.where(low, cp, gp)
-        strips[0, 1, rows, :] = jnp.where(low, gp, cp)
-        strips[1, 0, rows, :] = jnp.where(low, cu, gu)
-        strips[1, 1, rows, :] = jnp.where(low, gu, cu)
+        strips[0][rows, :] = jnp.where(low, cp, gp)
+        strips[1][rows, :] = jnp.where(low, gp, cp)
+        strips[2][rows, :] = jnp.where(low, cu, gu)
+        strips[3][rows, :] = jnp.where(low, gu, cu)
 
     def aniso_of(dz, dy, dx):
         sz, sy, sx = dz * dz, dy * dy, dx * dx
@@ -243,12 +267,12 @@
     strip_thermal = thermal_of(DEPTH * gz + q_lane)
 
     def strip_near(field, side, r0):
-        v = strips[field, side, r0 : r0 + 8, :]
+        v = strips[2 * field + side][r0 : r0 + 8, :]
         return v, (
             pltpu.roll(v, 120, 1),
             pltpu.roll(v, 8, 1),
-            strips[field, side, r0 + 1 : r0 + 9, :],
-            strips[field, side, r0 - 1 : r0 + 7, :],
+            strips[2 * field + side][r0 + 1 : r0 + 9, :],
+            strips[2 * field + side][r0 - 1 : r0 + 7, :],
             pltpu.roll(v, 127, 1),
             pltpu.roll(v, 1, 1),
         )
@@ -256,85 +280,96 @@
     def strip_stage(fn, edge):
         for t in range(TILES):
             r0 = 8 + 8 * t
-            left = fn(0, r0)
-            right = fn(1, r0)
-            edges[edge, r0 : r0 + 8, :] = jnp.where(low, left, right)
+            edges[edge][r0 : r0 + 8, :] = jnp.where(low, fn(0, r0), fn(1, r0))
 
     def strip_aniso(side, r0):
         _, n = strip_near(0, side, r0)
         a = aniso_of(n[0] - n[1], n[2] - n[3], n[4] - n[5])
-        strips[2, side, r0 : r0 + 8, :] = a
+        strips[4 + side][r0 : r0 + 8, :] = a
         return a
 
     def strip_phase(side, r0):
         p, ps = strip_near(0, side, r0)
         a, as_ = strip_near(2, side, r0)
-        u = strips[1, side, r0 : r0 + 8, :]
+        u = strips[2 + side][r0 : r0 + 8, :]
         n, d, r = phase_of(p, a, u, flux_sum(p, a, ps, as_), strip_thermal)
-        strips[3, side, r0 : r0 + 8, :] = n
-        strips[4, side, r0 : r0 + 8, :] = d
-        strips[5, side, r0 : r0 + 8, :] = r
+        strips[6 + side][r0 : r0 + 8, :] = n
+        strips[8 + side][r0 : r0 + 8, :] = d
+        strips[10 + side][r0 : r0 + 8, :] = r
         return n
 
     def strip_solute(side, r0):
         u, us = strip_near(1, side, r0)
         n, ns = strip_near(3, side, r0)
-        d = strips[4, side, r0 : r0 + 8, :]
-        r = strips[5, side, r0 : r0 + 8, :]
+        d = strips[8 + side][r0 : r0 + 8, :]
+        r = strips[10 + side][r0 : r0 + 8, :]
         return solute_of(u, d, r, flux_sum(u, n, us, ns))
 
     strip_stage(strip_aniso, 2)
     strip_stage(strip_phase, 3)
     strip_stage(strip_solute, 4)
-
-    def near(buf, edge, q, r0):
+    for edge in edges:
+        for t in range(TILES):
+            v = edge[8 + 8 * t : 16 + 8 * t, :]
+            edge[8 + 8 * t : 16 + 8 * t, :] = jnp.where(low, pltpu.roll(v, 127, 1), pltpu.roll(v, 1, 1))
+
+    def near(buf, edge, q, r0, kept=None, keep=None):
         p = q & 15
-        v = buf[p, r0 : r0 + 8, :]
-        e = pltpu.roll(edges[edge, r0 : r0 + 8, :], 124 - 8 * p, 1)
+        v = buf[p, pl.ds(r0, 8), :]
+        if kept is None:
+            e = pltpu.roll(edges[edge][pl.ds(r0, 8), :], 124 - 8 * p, 1)
+            right = jnp.where(at127, e, pltpu.roll(v, 127, 1))
+            left = jnp.where(at0, e, pltpu.roll(v, 1, 1))
+        else:
+            right = kept[0][p, pl.ds(r0, 8), :]
+            left = kept[1][p, pl.ds(r0, 8), :]
+        if keep is not None:
+            keep[0][p, pl.ds(r0, 8), :] = right
+            keep[1][p, pl.ds(r0, 8), :] = left
         return v, (
-            buf[(q + 1) & 15, r0 : r0 + 8, :],
-            buf[(q - 1) & 15, r0 : r0 + 8, :],
-            buf[p, r0 + 1 : r0 + 9, :],
-            buf[p, r0 - 1 : r0 + 7, :],
-            pltpu.roll(jnp.where(at0, e, v), 127, 1),
-            pltpu.roll(jnp.where(at127, e, v), 1, 1),
+            buf[(q + 1) & 15, pl.ds(r0, 8), :],
+            buf[(q - 1) & 15, pl.ds(r0, 8), :],
+            buf[p, pl.ds(r0 + 1, 8), :],
+            buf[p, pl.ds(r0 - 1, 8), :],
+            right,
+            left,
         )
 
-    def stage(first, count, tiles, fn):
+    def stage(first, count, tiles, fn, unroll=2):
         def step(i, carry):
             for t in tiles:
                 fn(shift + first + i, 8 + 8 * t)
             return carry
 
-        lax.fori_loop(0, count, step, 0)
+        lax.fori_loop(0, count, step, 0, unroll=unroll)
 
     def plane_aniso(q, r0):
-        _, n = near(pb, 0, q, r0)
-        ab[q & 15, r0 : r0 + 8, :] = aniso_of(n[0] - n[1], n[2] - n[3], n[4] - n[5])
+        _, n = near(pb, 0, q, r0, keep=(pr_b, pl_b))
+        ab[q & 15, pl.ds(r0, 8), :] = aniso_of(n[0] - n[1], n[2] - n[3], n[4] - n[5])
 
     def plane_phase(q, r0):
-        p, ps = near(pb, 0, q, r0)
+        p, ps = near(pb, 0, q, r0, kept=(pr_b, pl_b))
         a, as_ = near(ab, 2, q, r0)
-        u = ub[q & 15, r0 : r0 + 8, :]
+        u = ub[q & 15, pl.ds(r0, 8), :]
         n, d, r = phase_of(p, a, u, flux_sum(p, a, ps, as_), thermal_of(DEPTH * gz + q))
-        nb[q & 15, r0 : r0 + 8, :] = n
-        db[q & 15, r0 : r0 + 8, :] = d
-        rb[q & 15, r0 : r0 + 8, :] = r
-
-    def substep(buf, edge, q, r0):
+        nb[q & 15, pl.ds(r0, 8), :] = n
+        db[q & 15, pl.ds(r0, 8), :] = d
+        rb[q & 15, pl.ds(r0, 8), :] = r
+
+    def substep(buf, edge, q, r0, **held):
         u, us = near(buf, edge, q, r0)
-        n, ns = near(nb, 3, q, r0)
-        return n, solute_of(u, db[q & 15, r0 : r0 + 8, :], rb[q & 15, r0 : r0 + 8, :], flux_sum(u, n, us, ns))
+        n, ns = near(nb, 3, q, r0, **held)
+        return n, solute_of(u, db[q & 15, pl.ds(r0, 8), :], rb[q & 15, pl.ds(r0, 8), :], flux_sum(u, n, us, ns))
 
     def plane_first(q, r0):
-        _, v = substep(ub, 1, q, r0)
-        sb[q & 15, r0 : r0 + 8, :] = v
+        _, v = substep(ub, 1, q, r0, keep=(nr_b, nl_b))
+        sb[q & 15, pl.ds(r0, 8), :] = v
 
     def plane_second(q, r0):
-        n, v = substep(sb, 4, q, r0)
+        n, v = substep(sb, 4, q, r0, kept=(nr_b, nl_b))
         outside = DEPTH * gz + q >= total
-        phase_ref[q - shift, r0 - 16 : r0 - 8, :] = jnp.where(outside, -1.0, 1.0 - n)
-        solute_ref[q - shift, r0 - 16 : r0 - 8, :] = jnp.where(outside, 0.0, v)
+        phase_ref[q - shift, pl.ds(r0 - 16, 8), :] = jnp.where(outside, -1.0, 1.0 - n)
+        solute_ref[q - shift, pl.ds(r0 - 16, 8), :] = jnp.where(outside, 0.0, v)
 
     every = range(TILES)
     stage(-3, 14, every, plane_aniso)
@@ -364,16 +399,21 @@
     )(*args)
 
 
+def step_scratch():
+    return [pltpu.VMEM((16, ROWS, 128), F32)] * 11 + [pltpu.VMEM((ROWS, 128), F32)] * 17
+
+
 def branch(early, phase, solute, info):
-    near_p = moved(phase[0:7] if early else phase, "gz", -1)
-    near_u = moved(solute[0:5] if early else solute, "gz", -1)
-    if early:
-        extra = moved(jnp.concatenate([phase[5:8], solute[7:8]]), "gz", 1)
-    else:
-        extra = moved(jnp.concatenate([phase[0:4], solute[0:2]]), "gz", -2)
     own_c, up8, down8 = call(pack_kernel, (out(128, 128), out(8, 8, 128), out(8, 8, 128)), 0, phase, solute)
     left = moved(own_c, "gx", 1)
     right = moved(own_c, "gx", -1)
+    left, right, p, u = lax.optimization_barrier((left, right, phase, solute))
+    near_p = moved(p[0:7] if early else p, "gz", -1)
+    near_u = moved(u[0:5] if early else u, "gz", -1)
+    if early:
+        extra = moved(jnp.concatenate([p[5:8], u[7:8]]), "gz", 1)
+    else:
+        extra = moved(jnp.concatenate([p[0:4], u[0:2]]), "gz", -2)
     strip, up, down = call(
         strips_kernel, (out(128, 128), out(9, 8, 128), out(9, 8, 128)), 1, info, own_c, left, right, up8, down8
     )
@@ -382,7 +422,6 @@
     halo = call(halo_kernel, out(33, 8, 128), 1, info, from_up, from_down, up, down, strip)
     near_h = moved(halo, "gz", -1)
     extra_h = moved(halo, "gz", 1 if early else -2)
-    whole = pltpu.VMEM((16, ROWS, 128), F32)
     return call(
         functools.partial(step_kernel, early),
         (out(*phase.shape), out(*phase.shape)),
@@ -396,7 +435,7 @@
         halo,
         near_h,
         extra_h,
-        scratch=[whole] * 7 + [pltpu.VMEM((5, ROWS, 128), F32), pltpu.VMEM((6, 2, ROWS, 128), F32)],
+        scratch=step_scratch(),
     )
 
 

time: 74.5 us -> 58.5 us (0.79)
  the two profiles are of different devices: /device:TPU:122 before, /device:TPU:118 now
where the time goes in v2:
time: 58.5 us; the launch traced here: 58.2 us
  starting transfers between devices  30.1 us (51%)
  waiting for transfers between devices  14.8 us (25%)
  Pallas kernels  11.6 us (20%)
  between operations  1.29 us (2%)
    ppermute x9, starting transfers between devices, moved(): lax.ppermute(value, axis, [(source, source + steps) for source in range(f...  30.1 us
    ppermute x9, waiting for transfers between devices, moved(): lax.ppermute(value, axis, [(source, source + steps) for source in range(f...  14.8 us
    pallas_call x4, Pallas kernels, call(): pl.pallas_call(kernel, out_shape=shapes, in_specs=[SMEM] * n_smem + [VMEM...  11.6 us
  transfers between devices with their start and end apart: 9, of which 4 were waited for; matrix products, arithmetic and copies ran while one was open for 0% of the time, Pallas kernels for 2%

profile of v2, /device:TPU:118, one launch (start us, length us, event | category | flops | bytes accessed | tf_op | source)
XLA Modules:
  0.0 58.2 jit_solution(17920493055224380793)
XLA Ops:
  1.3 0.1 stack.15
  1.4 56.8 %conditional.1 = ((f32[8,128,128]{2,1,0:T(8,128)}, f32[8,128,128]{2,1,0:T(8,128)})) conditional(s32[]{:T(128)} %bitcast, (f32[8,128,128]{2,1,0:T(8,128)}, f32[8,128,128]{2,1,0:T(8,128)}, s32[7]{0:T(128)S(1)}) %tuple.15, (f32[8,128,128]{2,1,0:T(8,128)}, f32[8,128,128]{2,1,0:T(8,128)}, s32[7]{0:T(128)S(1)}) %tuple.15), branch_computations={%region_0.0_spmd, %region_1.0_spmd} | conditional | flops 98304 | bytes 13435304 | solution.py:447
  1.4 1.6 %branch_1_fun.4 = (f32[128,128]{1,0:T(8,128)S(1)}, f32[8,8,128]{2,1,0:T(8,128)S(1)}, f32[8,8,128]{2,1,0:T(8,128)S(1)}) custom-call(f32[8,128,128]{2,1,0:T(8,128)} %get-tuple-element.29.p_ref, f32[8,128,128]{2,1,0:T(8,128)} %get-tuple-element.30.u_ref), custom_call_target="tpu_custom_call" | custom-call | tf_op jit(solution)/shard_map/cond/branch_1_fun/pallas_call | solution.py:392
  3.0 0.0 copy-start.3
  3.0 2.3 %collective-permute-start.10 = (f32[128,128]{1,0:T(8,128)S(1)}, f32[128,128]{1,0:T(8,128)S(1)}, u32[]{:S(2)}, u32[]{:S(2)}) collective-permute-start(f32[128,128]{1,0:T(8,128)S(1)} %get-tuple-element.28.c_ref), channel_id=1, source_target_pairs={{1,0},{2,1},{3,2},{5,4},{6,5},{7,6},{9,8},{10,9},{11,10},{13,12},{... | collective-permute-start | bytes 196616 | tf_op jit(solution)/shard_map/cond/branch_1_fun/ppermute | solution.py:384
  5.3 2.1 %collective-permute-start.9 = (f32[128,128]{1,0:T(8,128)S(1)}, f32[128,128]{1,0:T(8,128)S(1)}, u32[]{:S(2)}, u32[]{:S(2)}) collective-permute-start(f32[128,128]{1,0:T(8,128)S(1)} %get-tuple-element.28.c_ref), channel_id=1, source_target_pairs={{0,1},{1,2},{2,3},{4,5},{5,6},{6,7},{8,9},{9,10},{10,11},{12,13},{... | collective-permute-start | bytes 196616 | tf_op jit(solution)/shard_map/cond/branch_1_fun/ppermute | solution.py:384
  7.5 0.0 collective-permute-done.10.right_ref
  7.5 3.4 %collective-permute-done.9.left_ref = f32[128,128]{1,0:T(8,128)S(1)} collective-permute-done((f32[128,128]{1,0:T(8,128)S(1)}, f32[128,128]{1,0:T(8,128)S(1)}, u32[]{:S(2)}, u32[]{:S(2)}) %collective-permute-start.9) | collective-permute-done | bytes 65568 | tf_op jit(solution)/shard_map/cond/branch_1_fun/ppermute | solution.py:384
  10.9 3.1 %collective-permute-start.11 = (f32[7,128,128]{2,1,0:T(8,128)S(1)}, f32[7,128,128]{2,1,0:T(8,128)S(1)}, u32[]{:S(2)}, u32[]{:S(2)}) collective-permute-start(f32[7,128,128]{2,1,0:T(8,128)S(1)} %slice.14), channel_id=1, source_target_pairs={{32,0},{64,32},{96,64},{128,96},{160,128},{192,160},{224,192},{33,... | collective-permute-start | bytes 1376264 | tf_op jit(solution)/shard_map/cond/branch_1_fun/ppermute | solution.py:384
  14.1 4.2 %collective-permute-start.12 = (f32[5,128,128]{2,1,0:T(8,128)S(1)}, f32[5,128,128]{2,1,0:T(8,128)S(1)}, u32[]{:S(2)}, u32[]{:S(2)}) collective-permute-start(f32[5,128,128]{2,1,0:T(8,128)S(1)} %slice.15), channel_id=1, source_target_pairs={{32,0},{64,32},{96,64},{128,96},{160,128},{192,160},{224,192},{33,... | collective-permute-start | bytes 983048 | tf_op jit(solution)/shard_map/cond/branch_1_fun/ppermute | solution.py:384
  18.3 4.1 %collective-permute-start.13 = (f32[4,128,128]{2,1,0:T(8,128)S(1)}, f32[4,128,128]{2,1,0:T(8,128)S(1)}, u32[]{:S(2)}, u32[]{:S(2)}) collective-permute-start(f32[4,128,128]{2,1,0:T(8,128)S(1)} %pad_maximum_fusion.1), channel_id=1, source_target_pairs={{0,32},{32,64},{64,96},{96,128},{128,160},{160,192},{192,224},{1,3... | collective-permute-start | bytes 786440 | tf_op jit(solution)/shard_map/cond/branch_1_fun/ppermute | solution.py:384
  22.4 0.8 %branch_1_fun.5 = (f32[128,128]{1,0:T(8,128)S(1)}, f32[9,8,128]{2,1,0:T(8,128)S(1)}, f32[9,8,128]{2,1,0:T(8,128)S(1)}) custom-call(s32[7]{0:T(128)S(1)} %get-tuple-element.25.info_ref, f32[128,128]{1,0:T(8,128)S(1)} %get-tuple-element.28.c_ref, f32[128,128]{1,0:T(8,128)S(1)} %collective-permute-done.9.left_ref, ...), custom_call_target="tpu_custom_call" | custom-call | tf_op jit(solution)/shard_map/cond/branch_1_fun/pallas_call | solution.py:392
  23.2 5.0 %collective-permute-start.14 = (f32[9,8,128]{2,1,0:T(8,128)S(1)}, f32[9,8,128]{2,1,0:T(8,128)S(1)}, u32[]{:S(2)}, u32[]{:S(2)}) collective-permute-start(f32[9,8,128]{2,1,0:T(8,128)S(1)} %get-tuple-element.35.up_ref), channel_id=1, source_target_pairs={{0,4},{4,8},{8,12},{12,16},{16,20},{20,24},{24,28},{1,5},{5,9},{9,... | collective-permute-start | bytes 110600 | tf_op jit(solution)/shard_map/cond/branch_1_fun/ppermute | solution.py:384
  28.2 1.9 %collective-permute-start.15 = (f32[9,8,128]{2,1,0:T(8,128)S(1)}, f32[9,8,128]{2,1,0:T(8,128)S(1)}, u32[]{:S(2)}, u32[]{:S(2)}) collective-permute-start(f32[9,8,128]{2,1,0:T(8,128)S(1)} %get-tuple-element.36.down_ref), channel_id=1, source_target_pairs={{4,0},{8,4},{12,8},{16,12},{20,16},{24,20},{28,24},{5,1},{9,5},{13... | collective-permute-start | bytes 110600 | tf_op jit(solution)/shard_map/cond/branch_1_fun/ppermute | solution.py:384
  30.1 0.0 collective-permute-done.14.from_up_ref
  30.1 5.1 %collective-permute-done.15.from_down_ref = f32[9,8,128]{2,1,0:T(8,128)S(1)} collective-permute-done((f32[9,8,128]{2,1,0:T(8,128)S(1)}, f32[9,8,128]{2,1,0:T(8,128)S(1)}, u32[]{:S(2)}, u32[]{:S(2)}) %collective-permute-start.15) | collective-permute-done | bytes 36896 | tf_op jit(solution)/shard_map/cond/branch_1_fun/ppermute | solution.py:384
  35.3 0.6 branch_1_fun.6.h_ref
  35.8 4.3 %collective-permute-start.17 = (f32[33,8,128]{2,1,0:T(8,128)S(1)}, f32[33,8,128]{2,1,0:T(8,128)S(1)}, u32[]{:S(2)}, u32[]{:S(2)}) collective-permute-start(f32[33,8,128]{2,1,0:T(8,128)S(1)} %branch_1_fun.6.h_ref), channel_id=1, source_target_pairs={{0,32},{32,64},{64,96},{96,128},{128,160},{160,192},{192,224},{1,3... | collective-permute-start | bytes 405512 | tf_op jit(solution)/shard_map/cond/branch_1_fun/ppermute | solution.py:384
  40.1 3.0 %collective-permute-start.16 = (f32[33,8,128]{2,1,0:T(8,128)S(1)}, f32[33,8,128]{2,1,0:T(8,128)S(1)}, u32[]{:S(2)}, u32[]{:S(2)}) collective-permute-start(f32[33,8,128]{2,1,0:T(8,128)S(1)} %branch_1_fun.6.h_ref), channel_id=1, source_target_pairs={{32,0},{64,32},{96,64},{128,96},{160,128},{192,160},{224,192},{33,... | collective-permute-start | bytes 405512 | tf_op jit(solution)/shard_map/cond/branch_1_fun/ppermute | solution.py:384
  43.2 1.1 %collective-permute-done.17.hx_ref = f32[33,8,128]{2,1,0:T(8,128)S(1)} collective-permute-done((f32[33,8,128]{2,1,0:T(8,128)S(1)}, f32[33,8,128]{2,1,0:T(8,128)S(1)}, u32[]{:S(2)}, u32[]{:S(2)}) %collective-permute-start.17) | collective-permute-done | bytes 135200 | tf_op jit(solution)/shard_map/cond/branch_1_fun/ppermute | solution.py:384
  44.3 5.2 %collective-permute-done.16.hn_ref = f32[33,8,128]{2,1,0:T(8,128)S(1)} collective-permute-done((f32[33,8,128]{2,1,0:T(8,128)S(1)}, f32[33,8,128]{2,1,0:T(8,128)S(1)}, u32[]{:S(2)}, u32[]{:S(2)}) %collective-permute-start.16) | collective-permute-done | bytes 135200 | tf_op jit(solution)/shard_map/cond/branch_1_fun/ppermute | solution.py:384
  49.5 0.0 collective-permute-done.13.ex_ref
  49.5 0.0 collective-permute-done.12.un_ref
  49.5 8.7 %branch_1_fun.7 = (f32[8,128,128]{2,1,0:T(8,128)}, f32[8,128,128]{2,1,0:T(8,128)}) custom-call(s32[7]{0:T(128)S(1)} %get-tuple-element.25.info_ref, f32[8,128,128]{2,1,0:T(8,128)S(1)} %copy-done.1, f32[8,128,128]{2,1,0:T(8,128)S(1)} %copy-done.3, f32[7,128,128]{2,1,0:T(8,128)S(1)} %collective-permute-done.11.pn_ref, ...), custom_call_target="tpu_custom_call" | custom-call | tf_op jit(solution)/shard_map/cond/branch_1_fun/pallas_call | solution.py:392
  (10 shorter events, 0.1 us)
Async XLA Ops:
  1.4 9.5 %copy-start.1 = (f32[8,128,128]{2,1,0:T(8,128)S(1)}, f32[8,128,128]{2,1,0:T(8,128)}, u32[]{:S(2)}) copy-start(f32[8,128,128]{2,1,0:T(8,128)} %get-tuple-element.29.p_ref) | copy-start | bytes 1572868 | tf_op jit(solution)/shard_map/cond
  3.0 11.0 %copy-start.3 = (f32[8,128,128]{2,1,0:T(8,128)S(1)}, f32[8,128,128]{2,1,0:T(8,128)}, u32[]{:S(2)}) copy-start(f32[8,128,128]{2,1,0:T(8,128)} %get-tuple-element.30.u_ref) | copy-start | bytes 1572868 | tf_op jit(solution)/shard_map/cond
  3.0 4.5 %collective-permute-start.10 = (f32[128,128]{1,0:T(8,128)S(1)}, f32[128,128]{1,0:T(8,128)S(1)}, u32[]{:S(2)}, u32[]{:S(2)}) collective-permute-start(f32[128,128]{1,0:T(8,128)S(1)} %get-tuple-element.28.c_ref), channel_id=1, source_target_pairs={{1,0},{2,1},{3,2},{5,4},{6,5},{7,6},{9,8},{10,9},{11,10},{13,12},{... | collective-permute-start | bytes 196616 | tf_op jit(solution)/shard_map/cond/branch_1_fun/ppermute | solution.py:384
  5.3 5.6 %collective-permute-start.9 = (f32[128,128]{1,0:T(8,128)S(1)}, f32[128,128]{1,0:T(8,128)S(1)}, u32[]{:S(2)}, u32[]{:S(2)}) collective-permute-start(f32[128,128]{1,0:T(8,128)S(1)} %get-tuple-element.28.c_ref), channel_id=1, source_target_pairs={{0,1},{1,2},{2,3},{4,5},{5,6},{6,7},{8,9},{9,10},{10,11},{12,13},{... | collective-permute-start | bytes 196616 | tf_op jit(solution)/shard_map/cond/branch_1_fun/ppermute | solution.py:384
  10.9 38.5 %collective-permute-start.11 = (f32[7,128,128]{2,1,0:T(8,128)S(1)}, f32[7,128,128]{2,1,0:T(8,128)S(1)}, u32[]{:S(2)}, u32[]{:S(2)}) collective-permute-start(f32[7,128,128]{2,1,0:T(8,128)S(1)} %slice.14), channel_id=1, source_target_pairs={{32,0},{64,32},{96,64},{128,96},{160,128},{192,160},{224,192},{33,... | collective-permute-start | bytes 1376264 | tf_op jit(solution)/shard_map/cond/branch_1_fun/ppermute | solution.py:384
  14.1 35.4 %collective-permute-start.12 = (f32[5,128,128]{2,1,0:T(8,128)S(1)}, f32[5,128,128]{2,1,0:T(8,128)S(1)}, u32[]{:S(2)}, u32[]{:S(2)}) collective-permute-start(f32[5,128,128]{2,1,0:T(8,128)S(1)} %slice.15), channel_id=1, source_target_pairs={{32,0},{64,32},{96,64},{128,96},{160,128},{192,160},{224,192},{33,... | collective-permute-start | bytes 983048 | tf_op jit(solution)/shard_map/cond/branch_1_fun/ppermute | solution.py:384
  18.3 31.2 %collective-permute-start.13 = (f32[4,128,128]{2,1,0:T(8,128)S(1)}, f32[4,128,128]{2,1,0:T(8,128)S(1)}, u32[]{:S(2)}, u32[]{:S(2)}) collective-permute-start(f32[4,128,128]{2,1,0:T(8,128)S(1)} %pad_maximum_fusion.1), channel_id=1, source_target_pairs={{0,32},{32,64},{64,96},{96,128},{128,160},{160,192},{192,224},{1,3... | collective-permute-start | bytes 786440 | tf_op jit(solution)/shard_map/cond/branch_1_fun/ppermute | solution.py:384
  23.2 7.0 %collective-permute-start.14 = (f32[9,8,128]{2,1,0:T(8,128)S(1)}, f32[9,8,128]{2,1,0:T(8,128)S(1)}, u32[]{:S(2)}, u32[]{:S(2)}) collective-permute-start(f32[9,8,128]{2,1,0:T(8,128)S(1)} %get-tuple-element.35.up_ref), channel_id=1, source_target_pairs={{0,4},{4,8},{8,12},{12,16},{16,20},{20,24},{24,28},{1,5},{5,9},{9,... | collective-permute-start | bytes 110600 | tf_op jit(solution)/shard_map/cond/branch_1_fun/ppermute | solution.py:384
  28.2 7.1 %collective-permute-start.15 = (f32[9,8,128]{2,1,0:T(8,128)S(1)}, f32[9,8,128]{2,1,0:T(8,128)S(1)}, u32[]{:S(2)}, u32[]{:S(2)}) collective-permute-start(f32[9,8,128]{2,1,0:T(8,128)S(1)} %get-tuple-element.36.down_ref), channel_id=1, source_target_pairs={{4,0},{8,4},{12,8},{16,12},{20,16},{24,20},{28,24},{5,1},{9,5},{13... | collective-permute-start | bytes 110600 | tf_op jit(solution)/shard_map/cond/branch_1_fun/ppermute | solution.py:384
  35.8 8.5 %collective-permute-start.17 = (f32[33,8,128]{2,1,0:T(8,128)S(1)}, f32[33,8,128]{2,1,0:T(8,128)S(1)}, u32[]{:S(2)}, u32[]{:S(2)}) collective-permute-start(f32[33,8,128]{2,1,0:T(8,128)S(1)} %branch_1_fun.6.h_ref), channel_id=1, source_target_pairs={{0,32},{32,64},{64,96},{96,128},{128,160},{160,192},{192,224},{1,3... | collective-permute-start | bytes 405512 | tf_op jit(solution)/shard_map/cond/branch_1_fun/ppermute | solution.py:384
  40.1 9.3 %collective-permute-start.16 = (f32[33,8,128]{2,1,0:T(8,128)S(1)}, f32[33,8,128]{2,1,0:T(8,128)S(1)}, u32[]{:S(2)}, u32[]{:S(2)}) collective-permute-start(f32[33,8,128]{2,1,0:T(8,128)S(1)} %branch_1_fun.6.h_ref), channel_id=1, source_target_pairs={{32,0},{64,32},{96,64},{128,96},{160,128},{192,160},{224,192},{33,... | collective-permute-start | bytes 405512 | tf_op jit(solution)/shard_map/cond/branch_1_fun/ppermute | solution.py:384

commit v3 on v2

--- a/solution.py
+++ b/solution.py
@@ -50,9 +50,8 @@
     return r * (2.0 - v * r)
 
 
-def pack_kernel(p_ref, u_ref, c_ref, up_ref, down_ref):
+def pack_kernel(p_ref, u_ref, c_ref):
     group = lanes() >> 3
-    sub = sublanes()
     for t in range(16):
         acc = jnp.zeros((8, 128), F32)
         for f, ref in enumerate((p_ref, u_ref)):
@@ -60,12 +59,20 @@
                 v = pltpu.roll(ref[z, 8 * t : 8 * t + 8, :], 64 * f + 8 * z + 4, 1)
                 acc = jnp.where(group == 8 * f + z, v, acc)
         c_ref[8 * t : 8 * t + 8, :] = acc
+
+
+def rows_kernel(c_ref, p_ref, u_ref, up_ref, down_ref, m_ref):
+    sub = sublanes()
+    lane = lanes()
     for z in range(DEPTH):
         up_ref[z] = jnp.where(sub >= 4, p_ref[z, 120:128, :], pltpu.roll(u_ref[z, 120:128, :], 4, 0))
         down_ref[z] = jnp.where(sub < 4, p_ref[z, 0:8, :], pltpu.roll(u_ref[z, 0:8, :], 4, 0))
-
-
-def strips_kernel(info_ref, c_ref, left_ref, right_ref, up8_ref, down8_ref, s_ref, up_ref, down_ref):
+    for t in range(16):
+        rows = slice(8 * t, 8 * t + 8)
+        m_ref[rows, :] = reversed_bits(c_ref[rows, :], (1, 2, 4), 1, lane)
+
+
+def strips_kernel(info_ref, m_ref, left_ref, right_ref, up8_ref, down8_ref, s_ref, up_ref, down_ref):
     lane = lanes()
     low = (lane & 4) == 0
     first = info_ref[3] == 0
@@ -74,8 +81,7 @@
     for t in range(16):
         rows = slice(8 * t, 8 * t + 8)
         v = jnp.where(low, left_ref[rows, :], right_ref[rows, :])
-        own = reversed_bits(c_ref[rows, :], (1, 2, 4), 1, lane)
-        v = jnp.where(mirror, own, v)
+        v = jnp.where(mirror, m_ref[rows, :], v)
         s_ref[rows, :] = v
         if t == 0:
             down_ref[8] = v
@@ -103,17 +109,22 @@
         h_ref[16 + t] = s_ref[8 * t : 8 * t + 8, :]
 
 
+CLASSES = ((1, 5, 3, 3, 1), (2, 7, 5, 2, 0), (4, 8, 6, 0, 0), (5, 8, 8, 2, 0), (7, 8, 8, 4, 2))
+ORDER = [("p", z) for z in range(5)] + [("u", z) for z in range(3)]
+ORDER += [("p", 5), ("u", 3), ("p", 6), ("u", 4), ("p", 7), ("u", 5), ("u", 6), ("u", 7)]
+
+
 def step_kernel(
-    early,
+    kind,
     info_ref,
     p_ref,
     u_ref,
-    pn_ref,
-    un_ref,
+    next_ref,
+    rest_ref,
     ex_ref,
+    edge_ref,
     h_ref,
     hn_ref,
-    hx_ref,
     phase_ref,
     solute_ref,
     pb,
@@ -131,6 +142,9 @@
 ):
     edges, strips = more[:5], more[5:]
     shift = info_ref[0]
+    least, next_p, next_u, extra_p, extra_u = kind
+    early = least < 4
+    split = extra_p >= 3
     gz = info_ref[1]
     count_z = info_ref[4]
     total = DEPTH * count_z
@@ -143,44 +157,38 @@
     is_last = gz == count_z - 1
     is_second = gz == count_z - 2
 
-    def place(buf, pos, src, index, h, base):
-        buf[pos, 16:144, :] = src[index]
-        edge = h[base]
+    def place(buf, pos, plane, edge):
+        buf[pos, 16:144, :] = plane
         buf[pos, 8:16, :] = edge
         buf[pos, 144:152, :] = edge
 
-    extra_p = 3 if early else 4
-    extra_u = 1 if early else 2
+    def third(z):
+        return edge_ref[z] if split else ex_ref[16 * (extra_p + extra_u) + z]
+
     for z in range(DEPTH):
-        place(pb, z, p_ref, z, h_ref, z)
-        place(ub, z, u_ref, z, h_ref, 8 + z)
-    for z in range(pn_ref.shape[0]):
-        place(pb, 8 + z, pn_ref, z, hn_ref, z)
-    for z in range(un_ref.shape[0]):
-        place(ub, 8 + z, un_ref, z, hn_ref, 8 + z)
-    for j in range(extra_p):
-        pos = 13 + j if early else j
-        taken = pos >= 12 + shift if early else pos <= shift - 5
-
-        @pl.when(taken)
-        def _():
-            place(pb, pos, ex_ref, j, hx_ref, 5 + j if early else j)
-
-    for j in range(extra_u):
-        pos = 15 if early else j
-        taken = pos >= 14 + shift if early else pos <= shift - 7
-
-        @pl.when(taken)
-        def _():
-            place(ub, pos, ex_ref, extra_p + j, hx_ref, 8 + (7 if early else j))
-
-    for pos in (12, 13, 14, 15) if early else (0, 1, 2, 3):
-        taken = (pos >= 12 + shift) & is_first if early else (pos <= shift - 5) & is_second
-
-        @pl.when(taken)
-        def _():
-            pb[pos, 8:152, :] = pb[15 - pos, 8:152, :]
-            ub[pos, 8:152, :] = ub[15 - pos, 8:152, :]
+        place(pb, z, p_ref[z], h_ref[z])
+        place(ub, z, u_ref[z], h_ref[8 + z])
+    for i in range(next_p + next_u):
+        field, z = ORDER[i]
+        src = rest_ref[i - 8] if split and i >= 8 else next_ref[i]
+        place(pb if field == "p" else ub, 8 + z, src, hn_ref[z if field == "p" else 8 + z])
+
+    for buf, extra, base, margin in ((pb, extra_p, 0, 4), (ub, extra_u, extra_p, 2)):
+        for j in range(extra):
+            pos = 16 - extra + j if early else j
+            taken = pos >= 16 - margin + shift if early else pos <= shift + margin - 9
+
+            @pl.when(taken)
+            def _():
+                for t in range(16):
+                    buf[pos, 16 + 8 * t : 24 + 8 * t, :] = ex_ref[16 * (base + j) + t]
+                edge = third(base + j)
+                buf[pos, 8:16, :] = edge
+                buf[pos, 144:152, :] = edge
+
+            @pl.when(taken & (is_first if early else is_second))
+            def _():
+                buf[pos, 8:152, :] = buf[15 - pos, 8:152, :]
 
     @pl.when(is_last)
     def _():
@@ -188,22 +196,26 @@
             pb[pos, 8:152, :] = pb[15 - pos, 8:152, :]
             ub[pos, 8:152, :] = ub[15 - pos, 8:152, :]
 
-    fresh = group >= 12 + shift if early else group <= shift - 5
-    mirror = (is_last & (group >= 8) & (group < 12)) | (fresh & (is_first if early else is_second))
+    fresh = (group >= 12 + shift) if early else (group <= shift - 5)
+    beyond = is_first if early else is_second
+    mirror = (is_last & (group >= 8) & (group < 12)) | (fresh & beyond)
     for t in range(TILES):
-        src = 32 if t in (0, TILES - 1) else 15 + t
-        own, near, far = h_ref[src], hn_ref[src], hx_ref[src]
-        own_r, near_r, far_r = (pltpu.roll(v, 64, 1) for v in (own, near, far))
-        cp = jnp.where(group < 8, own, near_r)
-        cu = jnp.where(group < 8, own_r, near)
+        src = 16 if t in (0, TILES - 1) else t - 1
         rows = slice(8 + 8 * t, 16 + 8 * t)
-        edges[0][rows, :] = jnp.where(fresh, far_r if early else far, cp)
-        edges[1][rows, :] = jnp.where(fresh, far if early else far_r, cu)
-
-    @pl.when(is_last | (is_first if early else is_second))
+        own, near = h_ref[16 + src], hn_ref[16 + src]
+        cp = jnp.where(group < 8, own, pltpu.roll(near, 64, 1))
+        cu = jnp.where(group < 8, pltpu.roll(own, 64, 1), near)
+        if extra_p:
+            far = third(extra_p + extra_u + src)
+            far_r = pltpu.roll(far, 64, 1)
+            cp = jnp.where(fresh, far_r if early else far, cp)
+            cu = jnp.where(fresh, far if early else far_r, cu)
+        edges[0][rows, :] = cp
+        edges[1][rows, :] = cu
+
+    @pl.when(is_last | beyond)
     def _():
-        back = is_first if early else False
-        pick = (lane >> 3) & 3
+        pick = group & 3
         for t in range(TILES):
             rows = slice(8 + 8 * t, 16 + 8 * t)
             for field in (0, 1):
@@ -212,8 +224,8 @@
                 for j in range(4):
                     amount = 8 * (2 * j + 1)
                     if early:
-                        turned = pltpu.roll(v, jnp.where(back, 128 - amount, amount), 1)
-                        m = jnp.where(pick == jnp.where(back, 3 - j, j), turned, m)
+                        turned = pltpu.roll(v, jnp.where(is_first, 128 - amount, amount), 1)
+                        m = jnp.where(pick == jnp.where(is_first, 3 - j, j), turned, m)
                     else:
                         m = jnp.where(pick == j, pltpu.roll(v, amount, 1), m)
                 edges[field][rows, :] = jnp.where(mirror, m, v)
@@ -403,38 +415,51 @@
     return [pltpu.VMEM((16, ROWS, 128), F32)] * 11 + [pltpu.VMEM((ROWS, 128), F32)] * 17
 
 
-def branch(early, phase, solute, info):
-    own_c, up8, down8 = call(pack_kernel, (out(128, 128), out(8, 8, 128), out(8, 8, 128)), 0, phase, solute)
-    left = moved(own_c, "gx", 1)
-    right = moved(own_c, "gx", -1)
-    left, right, p, u = lax.optimization_barrier((left, right, phase, solute))
-    near_p = moved(p[0:7] if early else p, "gz", -1)
-    near_u = moved(u[0:5] if early else u, "gz", -1)
-    if early:
-        extra = moved(jnp.concatenate([p[5:8], u[7:8]]), "gz", 1)
+def branch(kind, phase, solute, planes, info, left, right, mirrored, up8, down8):
+    least, next_p, next_u, extra_p, extra_u = kind
+    early = least < 4
+    p = phase[DEPTH - extra_p :] if early else phase[:extra_p]
+    u = solute[DEPTH - extra_u :] if early else solute[:extra_u]
+    way = 1 if early else -2
+    split = extra_p >= 3
+    rest = planes[:1]
+    if split:
+        near = moved(planes[:8], "gz", -1)
+        if next_p + next_u > 8:
+            rest = moved(planes[8:], "gz", -1)
+        main = moved(jnp.concatenate([p, u]).reshape(-1, 8, 128), "gz", way)
     else:
-        extra = moved(jnp.concatenate([p[0:4], u[0:2]]), "gz", -2)
+        near = moved(planes[: next_p + next_u], "gz", -1)
     strip, up, down = call(
-        strips_kernel, (out(128, 128), out(9, 8, 128), out(9, 8, 128)), 1, info, own_c, left, right, up8, down8
+        strips_kernel, (out(128, 128), out(9, 8, 128), out(9, 8, 128)), 1, info, mirrored, left, right, up8, down8
     )
     from_up = moved(up, "gy", 1)
     from_down = moved(down, "gy", -1)
     halo = call(halo_kernel, out(33, 8, 128), 1, info, from_up, from_down, up, down, strip)
     near_h = moved(halo, "gz", -1)
-    extra_h = moved(halo, "gz", 1 if early else -2)
+    far = halo
+    edge = halo[:1]
+    if extra_p:
+        hp = halo[DEPTH - extra_p : DEPTH] if early else halo[:extra_p]
+        hu = halo[2 * DEPTH - extra_u : 2 * DEPTH] if early else halo[DEPTH : DEPTH + extra_u]
+        tiles = [hp, hu, halo[16:33]]
+        if split:
+            far, edge = main, moved(jnp.concatenate(tiles), "gz", way)
+        else:
+            far = moved(jnp.concatenate([v.reshape(-1, 8, 128) for v in (p, u)] + tiles), "gz", way)
     return call(
-        functools.partial(step_kernel, early),
+        functools.partial(step_kernel, kind),
         (out(*phase.shape), out(*phase.shape)),
         1,
         info,
         phase,
         solute,
-        near_p,
-        near_u,
-        extra,
+        near,
+        rest,
+        far,
+        edge,
         halo,
         near_h,
-        extra_h,
         scratch=step_scratch(),
     )
 
@@ -444,9 +469,16 @@
     info = jnp.stack(
         [advance[0]] + [lax.axis_index(a) for a in axes] + [jnp.int32(lax.axis_size(a)) for a in axes]
     ).astype(jnp.int32)
-    return lax.cond(
-        advance[0] < 4, functools.partial(branch, True), functools.partial(branch, False), phase, solute, info
+    own_c = call(pack_kernel, out(128, 128), 0, phase, solute)
+    left = moved(own_c, "gx", 1)
+    right = moved(own_c, "gx", -1)
+    up8, down8, mirrored = call(
+        rows_kernel, (out(8, 8, 128), out(8, 8, 128), out(128, 128)), 0, own_c, phase, solute
     )
+    planes = jnp.stack([(phase if field == "p" else solute)[z] for field, z in ORDER])
+    index = sum((advance[0] >= kind[0]).astype(jnp.int32) for kind in CLASSES[1:])
+    branches = [functools.partial(branch, kind) for kind in CLASSES]
+    return lax.switch(index, branches, phase, solute, planes, info, left, right, mirrored, up8, down8)
 
 
 def solution(mesh):

time: 58.5 us -> 55 us (0.940)
  the two profiles are of different devices: /device:TPU:118 before, /device:TPU:69 now
where the time goes in v3:
time: 55 us; the launch traced here: 54.7 us
  waiting for transfers between devices  24.6 us (45%)
  starting transfers between devices  16.7 us (30%)
  Pallas kernels  11.7 us (21%)
  between operations  1.43 us (3%)
    ppermute x7, waiting for transfers between devices, moved(): lax.ppermute(value, axis, [(source, source + steps) for source in range(f...  24.6 us
    ppermute x7, starting transfers between devices, moved(): lax.ppermute(value, axis, [(source, source + steps) for source in range(f...  16.7 us
    pallas_call x5, Pallas kernels, call(): pl.pallas_call(kernel, out_shape=shapes, in_specs=[SMEM] * n_smem + [VMEM...  11.7 us
  transfers between devices with their start and end apart: 7, of which 4 were waited for; matrix products, arithmetic and copies ran while one was open for 0% of the time, Pallas kernels for 2%

profile of v3, /device:TPU:69, one launch (start us, length us, event | category | flops | bytes accessed | tf_op | source)
XLA Modules:
  0.0 54.7 jit_solution(1485521909916455193)
XLA Ops:
  0.6 0.0 copy-start
  0.6 1.6 %shard_map.60.c_ref = f32[128,128]{1,0:T(8,128)S(1)} custom-call(f32[8,128,128]{2,1,0:T(8,128)} %p_ref.3, f32[8,128,128]{2,1,0:T(8,128)} %u_ref.3), custom_call_target="tpu_custom_call" | custom-call | tf_op jit(solution)/shard_map/pallas_call | solution.py:404
  2.2 0.0 copy-start.1
  2.2 2.7 %collective-permute-start.28 = (f32[128,128]{1,0:T(8,128)S(1)}, f32[128,128]{1,0:T(8,128)S(1)}, u32[]{:S(2)}, u32[]{:S(2)}) collective-permute-start(f32[128,128]{1,0:T(8,128)S(1)} %shard_map.60.c_ref), channel_id=1, source_target_pairs={{1,0},{2,1},{3,2},{5,4},{6,5},{7,6},{9,8},{10,9},{11,10},{13,12},{... | collective-permute-start | bytes 196616 | tf_op jit(solution)/shard_map/ppermute | solution.py:396
  5.0 3.0 %collective-permute-start.27 = (f32[128,128]{1,0:T(8,128)S(1)}, f32[128,128]{1,0:T(8,128)S(1)}, u32[]{:S(2)}, u32[]{:S(2)}) collective-permute-start(f32[128,128]{1,0:T(8,128)S(1)} %shard_map.60.c_ref), channel_id=1, source_target_pairs={{0,1},{1,2},{2,3},{4,5},{5,6},{6,7},{8,9},{9,10},{10,11},{12,13},{... | collective-permute-start | bytes 196616 | tf_op jit(solution)/shard_map/ppermute | solution.py:396
  8.0 0.0 copy-done
  8.1 0.2 shard_map.61
  9.1 0.1 stack.20
  9.1 0.0 collective-permute-done.28
  9.1 0.1 collective-permute-done.27
  9.3 45.5 %conditional.1 = ((f32[8,128,128]{2,1,0:T(8,128)}, f32[8,128,128]{2,1,0:T(8,128)})) conditional(s32[]{:T(128)} %bitcast.4, (f32[16,128,128]{2,1,0:T(8,128)S(1)}, f32[8,128,128]{2,1,0:T(8,128)S(1)}, f32[8,128,128]{2,1,0:T(8,128)S(1)}, s32[7]{0:T(128)S(1)}, f32[128,128]{1,0:T(8,128)S(1)}, ...), branch_computations={%region_0.0_spmd, %region_1.0_spmd, %region_2.0_spmd, %region_3.0_... | conditional | flops 145408 | bytes 11026720 | solution.py:481
  9.3 2.3 %collective-permute-start.15 = (f32[16,128,128]{2,1,0:T(8,128)S(1)}, f32[16,128,128]{2,1,0:T(8,128)S(1)}, u32[]{:S(2)}, u32[]{:S(2)}) collective-permute-start(f32[16,128,128]{2,1,0:T(8,128)S(1)} %get-tuple-element.140), channel_id=1, source_target_pairs={{32,0},{64,32},{96,64},{128,96},{160,128},{192,160},{224,192},{33,... | collective-permute-start | bytes 3145736 | tf_op jit(solution)/shard_map/cond/branch_3_fun/ppermute | solution.py:396
  11.6 0.6 %branch_3_fun.3 = (f32[128,128]{1,0:T(8,128)S(1)}, f32[9,8,128]{2,1,0:T(8,128)S(1)}, f32[9,8,128]{2,1,0:T(8,128)S(1)}) custom-call(s32[7]{0:T(128)S(1)} %get-tuple-element.137.info_ref, f32[128,128]{1,0:T(8,128)S(1)} %get-tuple-element.142.m_ref, f32[128,128]{1,0:T(8,128)S(1)} %get-tuple-element.143.left_ref, f32[128,128]{1,0:T(8,128)S(1)} %get-tuple-element.144.right_ref, ...), custom_call_target="tpu_custom_call" | custom-call | tf_op jit(solution)/shard_map/cond/branch_3_fun/pallas_call | solution.py:404
  12.2 3.5 %collective-permute-start.16 = (f32[9,8,128]{2,1,0:T(8,128)S(1)}, f32[9,8,128]{2,1,0:T(8,128)S(1)}, u32[]{:S(2)}, u32[]{:S(2)}) collective-permute-start(f32[9,8,128]{2,1,0:T(8,128)S(1)} %get-tuple-element.147.up_ref), channel_id=1, source_target_pairs={{0,4},{4,8},{8,12},{12,16},{16,20},{20,24},{24,28},{1,5},{5,9},{9,... | collective-permute-start | bytes 110600 | tf_op jit(solution)/shard_map/cond/branch_3_fun/ppermute | solution.py:396
  15.7 1.9 %collective-permute-start.17 = (f32[9,8,128]{2,1,0:T(8,128)S(1)}, f32[9,8,128]{2,1,0:T(8,128)S(1)}, u32[]{:S(2)}, u32[]{:S(2)}) collective-permute-start(f32[9,8,128]{2,1,0:T(8,128)S(1)} %get-tuple-element.148.down_ref), channel_id=1, source_target_pairs={{4,0},{8,4},{12,8},{16,12},{20,16},{24,20},{28,24},{5,1},{9,5},{13... | collective-permute-start | bytes 110600 | tf_op jit(solution)/shard_map/cond/branch_3_fun/ppermute | solution.py:396
  17.7 0.0 collective-permute-done.16.from_up_ref
  17.7 4.8 %collective-permute-done.17.from_down_ref = f32[9,8,128]{2,1,0:T(8,128)S(1)} collective-permute-done((f32[9,8,128]{2,1,0:T(8,128)S(1)}, f32[9,8,128]{2,1,0:T(8,128)S(1)}, u32[]{:S(2)}, u32[]{:S(2)}) %collective-permute-start.17) | collective-permute-done | bytes 36896 | tf_op jit(solution)/shard_map/cond/branch_3_fun/ppermute | solution.py:396
  22.4 0.6 %branch_3_fun.4.h_ref = f32[33,8,128]{2,1,0:T(8,128)S(1)} custom-call(s32[7]{0:T(128)S(1)} %get-tuple-element.137.info_ref, f32[9,8,128]{2,1,0:T(8,128)S(1)} %collective-permute-done.16.from_up_ref, f32[9,8,128]{2,1,0:T(8,128)S(1)} %collective-permute-done.17.from_down_ref, f32[9,8,128]{2,1,0:T(8,128)S(1)} %get-tuple-element.147.up_ref, ...), custom_call_target="tpu_custom_call" | custom-call | tf_op jit(solution)/shard_map/cond/branch_3_fun/pallas_call | solution.py:404
  23.1 1.3 %collective-permute-start.18 = (f32[51,8,128]{2,1,0:T(8,128)S(1)}, f32[51,8,128]{2,1,0:T(8,128)S(1)}, u32[]{:S(2)}, u32[]{:S(2)}) collective-permute-start(f32[51,8,128]{2,1,0:T(8,128)S(1)} %pad_maximum_fusion.3), channel_id=1, source_target_pairs={{64,0},{96,32},{128,64},{160,96},{192,128},{224,160},{65,1},{97,33... | collective-permute-start | bytes 626696 | tf_op jit(solution)/shard_map/cond/branch_3_fun/ppermute | solution.py:396
  24.4 1.9 %collective-permute-start.19 = (f32[33,8,128]{2,1,0:T(8,128)S(1)}, f32[33,8,128]{2,1,0:T(8,128)S(1)}, u32[]{:S(2)}, u32[]{:S(2)}) collective-permute-start(f32[33,8,128]{2,1,0:T(8,128)S(1)} %branch_3_fun.4.h_ref), channel_id=1, source_target_pairs={{32,0},{64,32},{96,64},{128,96},{160,128},{192,160},{224,192},{33,... | collective-permute-start | bytes 405512 | tf_op jit(solution)/shard_map/cond/branch_3_fun/ppermute | solution.py:396
  26.3 15.2 %collective-permute-done.19.hn_ref = f32[33,8,128]{2,1,0:T(8,128)S(1)} collective-permute-done((f32[33,8,128]{2,1,0:T(8,128)S(1)}, f32[33,8,128]{2,1,0:T(8,128)S(1)}, u32[]{:S(2)}, u32[]{:S(2)}) %collective-permute-start.19) | collective-permute-done | bytes 135200 | tf_op jit(solution)/shard_map/cond/branch_3_fun/ppermute | solution.py:396
  41.5 4.6 %collective-permute-done.18.ex_ref = f32[51,8,128]{2,1,0:T(8,128)S(1)} collective-permute-done((f32[51,8,128]{2,1,0:T(8,128)S(1)}, f32[51,8,128]{2,1,0:T(8,128)S(1)}, u32[]{:S(2)}, u32[]{:S(2)}) %collective-permute-start.18) | collective-permute-done | bytes 208928 | tf_op jit(solution)/shard_map/cond/branch_3_fun/ppermute | solution.py:396
  46.0 0.0 collective-permute-done.15.next_ref
  46.0 8.7 %branch_3_fun.5 = (f32[8,128,128]{2,1,0:T(8,128)}, f32[8,128,128]{2,1,0:T(8,128)}) custom-call(s32[7]{0:T(128)S(1)} %get-tuple-element.137.info_ref, f32[8,128,128]{2,1,0:T(8,128)S(1)} %get-tuple-element.138.p_ref, f32[8,128,128]{2,1,0:T(8,128)S(1)} %get-tuple-element.139.u_ref, f32[16,128,128]{2,1,0:T(8,128)S(1)} %collective-permute-done.15.next_ref, ...), custom_call_target="tpu_custom_call" | custom-call | tf_op jit(solution)/shard_map/cond/branch_3_fun/pallas_call | solution.py:404
  (15 shorter events, 0.1 us)
Async XLA Ops:
  0.6 7.3 %copy-start = (f32[8,128,128]{2,1,0:T(8,128)S(1)}, f32[8,128,128]{2,1,0:T(8,128)}, u32[]{:S(2)}) copy-start(f32[8,128,128]{2,1,0:T(8,128)} %p_ref.3) | copy-start | bytes 1572868
  2.2 5.8 %copy-start.1 = (f32[8,128,128]{2,1,0:T(8,128)S(1)}, f32[8,128,128]{2,1,0:T(8,128)}, u32[]{:S(2)}) copy-start(f32[8,128,128]{2,1,0:T(8,128)} %u_ref.3) | copy-start | bytes 1572868
  2.2 6.9 %collective-permute-start.28 = (f32[128,128]{1,0:T(8,128)S(1)}, f32[128,128]{1,0:T(8,128)S(1)}, u32[]{:S(2)}, u32[]{:S(2)}) collective-permute-start(f32[128,128]{1,0:T(8,128)S(1)} %shard_map.60.c_ref), channel_id=1, source_target_pairs={{1,0},{2,1},{3,2},{5,4},{6,5},{7,6},{9,8},{10,9},{11,10},{13,12},{... | collective-permute-start | bytes 196616 | tf_op jit(solution)/shard_map/ppermute | solution.py:396
  5.0 4.3 %collective-permute-start.27 = (f32[128,128]{1,0:T(8,128)S(1)}, f32[128,128]{1,0:T(8,128)S(1)}, u32[]{:S(2)}, u32[]{:S(2)}) collective-permute-start(f32[128,128]{1,0:T(8,128)S(1)} %shard_map.60.c_ref), channel_id=1, source_target_pairs={{0,1},{1,2},{2,3},{4,5},{5,6},{6,7},{8,9},{9,10},{10,11},{12,13},{... | collective-permute-start | bytes 196616 | tf_op jit(solution)/shard_map/ppermute | solution.py:396
  9.3 36.8 %collective-permute-start.15 = (f32[16,128,128]{2,1,0:T(8,128)S(1)}, f32[16,128,128]{2,1,0:T(8,128)S(1)}, u32[]{:S(2)}, u32[]{:S(2)}) collective-permute-start(f32[16,128,128]{2,1,0:T(8,128)S(1)} %get-tuple-element.140), channel_id=1, source_target_pairs={{32,0},{64,32},{96,64},{128,96},{160,128},{192,160},{224,192},{33,... | collective-permute-start | bytes 3145736 | tf_op jit(solution)/shard_map/cond/branch_3_fun/ppermute | solution.py:396
  12.2 5.5 %collective-permute-start.16 = (f32[9,8,128]{2,1,0:T(8,128)S(1)}, f32[9,8,128]{2,1,0:T(8,128)S(1)}, u32[]{:S(2)}, u32[]{:S(2)}) collective-permute-start(f32[9,8,128]{2,1,0:T(8,128)S(1)} %get-tuple-element.147.up_ref), channel_id=1, source_target_pairs={{0,4},{4,8},{8,12},{12,16},{16,20},{20,24},{24,28},{1,5},{5,9},{9,... | collective-permute-start | bytes 110600 | tf_op jit(solution)/shard_map/cond/branch_3_fun/ppermute | solution.py:396
  15.7 6.7 %collective-permute-start.17 = (f32[9,8,128]{2,1,0:T(8,128)S(1)}, f32[9,8,128]{2,1,0:T(8,128)S(1)}, u32[]{:S(2)}, u32[]{:S(2)}) collective-permute-start(f32[9,8,128]{2,1,0:T(8,128)S(1)} %get-tuple-element.148.down_ref), channel_id=1, source_target_pairs={{4,0},{8,4},{12,8},{16,12},{20,16},{24,20},{28,24},{5,1},{9,5},{13... | collective-permute-start | bytes 110600 | tf_op jit(solution)/shard_map/cond/branch_3_fun/ppermute | solution.py:396
  23.1 23.0 %collective-permute-start.18 = (f32[51,8,128]{2,1,0:T(8,128)S(1)}, f32[51,8,128]{2,1,0:T(8,128)S(1)}, u32[]{:S(2)}, u32[]{:S(2)}) collective-permute-start(f32[51,8,128]{2,1,0:T(8,128)S(1)} %pad_maximum_fusion.3), channel_id=1, source_target_pairs={{64,0},{96,32},{128,64},{160,96},{192,128},{224,160},{65,1},{97,33... | collective-permute-start | bytes 626696 | tf_op jit(solution)/shard_map/cond/branch_3_fun/ppermute | solution.py:396
  24.4 17.1 %collective-permute-start.19 = (f32[33,8,128]{2,1,0:T(8,128)S(1)}, f32[33,8,128]{2,1,0:T(8,128)S(1)}, u32[]{:S(2)}, u32[]{:S(2)}) collective-permute-start(f32[33,8,128]{2,1,0:T(8,128)S(1)} %branch_3_fun.4.h_ref), channel_id=1, source_target_pairs={{32,0},{64,32},{96,64},{128,96},{160,128},{192,160},{224,192},{33,... | collective-permute-start | bytes 405512 | tf_op jit(solution)/shard_map/cond/branch_3_fun/ppermute | solution.py:396
